TPU v7x, 32 devices: a whole 2x2x4 slice. The times are simulated.
32 devices in a mesh: frame: 4 (over y, x), space: 8 (over z, core).
Axes of the slice: x: 2, y: 2, z: 4, core: 2. Of those that a mesh axis runs over, the one named last changes fastest.
Arguments:
- qkv_now: bfloat16 [1024, 16, 384], P('space', 'frame'), as said below
- past_cache: bfloat16 [4, 1024, 16, 256], P('frame', 'space'), may hold values from -6 to 6
- frame_rank: int32 [4], replicated, may hold values from 0 to 3, each once
- frame_depth: int32 [8], replicated, may hold values from 0 to 4, as said below
- tile_lists: int32 [8, 8], replicated, may hold values from 0 to 1, as said below
Outputs:
- attended: bfloat16 [1024, 2048], P('space', 'frame')
Inputs may be any that keep to these rules, and one draw needn't show every extreme that they name: Entries of qkv_now lie within -5 to 5. `frame_depth`: some tile sees every past frame. `tile_lists`: entry [t, u] is 1 exactly where the distance between tiles t and u around the closed loop of 8 tiles is at most a radius of tile t; the diagonal is 1 and some tile sees all tiles.
All inputs are finite; a program needn't handle non-finite values.
Results may differ from a plain program's by a relative error of at most 0.01.
Values may be sent and summed in bfloat16 or wider, within the bound.
A program may use at most 64 MiB of HBM per device.

v0:
```python
import math

import jax
import jax.numpy as jnp
from jax import lax
from jax.sharding import PartitionSpec as P

NEG = -1e30


def body(qkv_now, past_cache, frame_rank, frame_depth, tile_lists):
    tok_rows = qkv_now.shape[0]
    head_count = qkv_now.shape[1]
    head_size = qkv_now.shape[2] // 3
    tiles = lax.axis_size("space")
    tile_index = lax.axis_index("space")
    score_scale = 1.0 / math.sqrt(head_size)
    total_rows = tok_rows * tiles
    tile_ids = jnp.arange(tiles, dtype=jnp.int32)
    past = lax.all_to_all(past_cache, "frame", split_axis=2, concat_axis=0, tiled=True)
    frame_count = past.shape[0]
    frame_seen = (frame_rank[None, :] >= frame_count - frame_depth[:, None]).astype(jnp.float32)
    my_column = lax.dynamic_index_in_dim(tile_lists, tile_index, 1, False).astype(jnp.float32)
    key_sets = jnp.concatenate(
        [past.reshape(frame_count * tok_rows, head_count, 2 * head_size), qkv_now[..., head_size:]],
        0,
    )
    seen_table = jnp.concatenate([frame_seen * my_column[:, None], my_column[:, None]], 1)
    groups = seen_table.shape[1]
    gathered = lax.all_gather(qkv_now[..., :head_size], "space", axis=0, tiled=True)
    block_rows = min(total_rows, 512)
    block_count = total_rows // block_rows
    blocks = gathered.reshape(block_count, block_rows, head_count, head_size)
    firsts = jnp.arange(block_count, dtype=jnp.int32) * block_rows

    def one_block(inputs):
        queries, first = inputs
        query_tiles = (first + jnp.arange(block_rows, dtype=jnp.int32)) // tok_rows
        onehot = (query_tiles[:, None] == tile_ids[None, :]).astype(jnp.float32)
        seen = jnp.dot(onehot, seen_table, preferred_element_type=jnp.float32)
        visible = jnp.broadcast_to(seen[:, :, None], (block_rows, groups, tok_rows)).reshape(
            block_rows, groups * tok_rows
        )
        scores = (
            jnp.einsum(
                "qhd,khd->hqk",
                queries,
                key_sets[..., :head_size],
                preferred_element_type=jnp.float32,
            )
            * score_scale
        )
        masked = jnp.where(visible[None] > 0, scores, NEG)
        peak = jnp.max(masked, axis=-1)
        weights = jnp.exp(masked - peak[..., None]) * visible[None]
        totals = jnp.sum(weights, axis=-1)
        weighted = jnp.einsum(
            "hqk,khd->qhd",
            weights.astype(jnp.bfloat16),
            key_sets[..., head_size:],
            preferred_element_type=jnp.float32,
        )
        safe = jnp.maximum(totals, 1.0).T
        share = (weighted / safe[..., None]).astype(jnp.bfloat16)
        return (share, peak.T + jnp.log(safe))

    shares, lse = lax.map(one_block, (blocks, firsts))
    shares = shares.reshape(total_rows, head_count, head_size)
    lse = lse.reshape(total_rows, head_count)
    overall = lax.pmax(lse, "space")
    factor = jnp.exp(lse - overall)
    scaled = shares.astype(jnp.float32) * factor[..., None]
    summed, denominator = (
        lax.psum_scatter(scaled, "space", scatter_dimension=0, tiled=True),
        lax.psum_scatter(factor, "space", scatter_dimension=0, tiled=True),
    )
    result = summed / denominator[..., None]
    return result.reshape(tok_rows, head_count * head_size).astype(jnp.bfloat16)


def solution(mesh):
    in_specs = (P("space", "frame", None), P("frame", "space", None, None), P(), P(), P())
    out_specs = P("space", "frame")
    return jax.shard_map(body, mesh=mesh, in_specs=in_specs, out_specs=out_specs, check_vma=False)
```

profile of v0, /device:TPU:0, one launch (start us, length us, event | category | flops | bytes accessed | tf_op | source)
XLA Modules:
  0.0 157.7 jit_solution(3267596829167493656)
XLA Ops:
  6.5 0.0 slice-start
  6.5 0.0 all-gather.2.cloned.1.call-start
  6.6 1.0 slice.18
  7.6 0.7 copy.40
  8.2 0.0 all-gather.2.cloned.1.call-update
  8.3 2.5 %copy.28 = bf16[1,128,16,256]{3,1,0,2:T(8,128)(2,1)} copy(bf16[1,128,16,256]{3,2,1,0:T(8,128)(2,1)} %param.8) | data formatting | bytes 2097152 | tf_op args[1]
  10.8 5.2 %all-to-all-start = ((bf16[1,128,16,256]{3,1,0,2:T(8,128)(2,1)}), bf16[1,128,16,256]{3,1,0,2:T(8,128)(2,1)S(1)}, u32[]{:S(2)}, u32[]{:S(2)}) async-start(bf16[1,128,16,256]{3,1,0,2:T(8,128)(2,1)} %copy.28), calls=%async_computation | async-start | bytes 2097152 | tf_op jit(solution)/shard_map/all_to_all | solution.py:20
  16.0 0.0 reduce-scatter.7.cloned.1.call-start
  16.0 0.0 slice-done
  16.0 0.0 copy-done.3
  16.1 0.2 fusion.32
  16.2 0.0 copy-done.5
  16.3 0.0 copy-done.4
  16.3 0.1 compare_select_fusion
  16.3 0.1 pad_maximum_fusion.1
  16.4 13.2 %all-to-all-done = bf16[1,128,16,256]{3,1,0,2:T(8,128)(2,1)S(1)} async-done(((bf16[1,128,16,256]{3,1,0,2:T(8,128)(2,1)}), bf16[1,128,16,256]{3,1,0,2:T(8,128)(2,1)S(1)}, u32[]{:S(2)}, u32[]{:S(2)}) %all-to-all-start) | async-done | bytes 1048608 | tf_op jit(solution)/shard_map/all_to_all | solution.py:20
  29.6 0.1 copy.29
  29.7 1.1 pad_maximum_fusion
  30.8 3.0 %all-gather.2.cloned.1.call-done = bf16[1024,4,128]{2,0,1:T(8,128)(2,1)} async-done(((bf16[128,4,128]{2,0,1:T(8,128)(2,1)}), bf16[1024,4,128]{2,0,1:T(8,128)(2,1)}) %all-gather.2.cloned.1.call-update) | async-done | bytes 1048592 | tf_op jit(solution)/shard_map/all_gather | solution.py:30
  33.8 21.2 %while.15 = (s32[]{:T(128)}, bf16[2,512,4,128]{3,1,0,2:T(8,128)(2,1)}, f32[2,512,4]{1,2,0:T(4,128)S(1)}, s32[2]{0:T(128)S(1)}, bf16[8,5]{1,0:T(8,128)(2,1)S(1)},...) while((s32[]{:T(128)}, bf16[2,512,4,128]{3,1,0,2:T(8,128)(2,1)}, ...), condition=%wide.region_3.4_spmd.clone, body=%wide.region_0.3_spmd.clone.sunk | while | flops 689035264 | bytes 40356124 | solution.py:67
  33.8 0.6 dynamic_slice.32
  34.4 0.7 add_select_fusion.2
  35.1 0.3 fusion.44
  35.4 0.1 bitcast_compare_fusion.2
  35.5 0.5 copy.44
  35.9 0.1 broadcast_in_dim.107
  36.1 0.4 copy.45
  36.5 0.0 copy-start
  36.5 0.0 copy-start.1
  36.5 2.7 %fusion.45 = (f32[4,512]{1,0:T(4,128)S(1)}, f32[4,512,640]{2,1,0:T(8,128)S(1)}) fusion(pred[512,640]{1,0:T(8,128)(4,1)S(1)} %copy.44, bf16[640,4,256]{2,0,1:T(8,128)(2,1)} %get-tuple-element.236, bf16[2,512,4,128]{3,1,0,2:T(8,128)(2,1)} %get-tuple-element.235, s32[]{:T(128)S(6)} %copy.51), kind=kOutput, calls=%fused_computation.3.clone.1 | convolution fusion | flops 339474432 | bytes 6758404 | tf_op jit(solution)/shard_map/while/body/eval_jaxpr/qhd,khd->hqk/dot_general | solution.py:45
  39.2 1.8 %fusion.46 = f32[4,512]{1,0:T(4,128)S(1)} fusion(f32[4,512,640]{2,1,0:T(8,128)S(1)} %get-tuple-element.212, f32[512,640]{1,0:T(8,128)S(1)} %copy.45, f32[4,512]{1,0:T(4,128)S(1)} %get-tuple-element.213, pred[512,640]{1,0:T(8,128)(4,1)S(1)} %copy.44), kind=kLoop, calls=%fused_computation.4.clone.1 | loop fusion | flops 6551552 | bytes 6897664 | tf_op jit(solution)/shard_map/while/body/eval_jaxpr/reduce_sum | solution.py:56
  41.0 0.0 copy-done
  41.0 0.0 copy-done.1
  41.0 2.4 %fusion.47 = bf16[2,512,4,128]{3,1,0,2:T(8,128)(2,1)S(1)} fusion(bf16[2,512,4,128]{3,1,0,2:T(8,128)(2,1)S(1)} %copy-done.1, s32[]{:T(128)S(6)} %copy.51, f32[4,512,640]{2,1,0:T(8,128)S(1)} %get-tuple-element.212, f32[512,640]{1,0:T(8,128)S(1)} %copy.45, f32[4,512]{1,0:T(4,128)S(1)} %get-tuple-element.213, pred[512,640]{1,0:T(8,128)(4,1)S(1)} %copy.44, ...), kind=kOutput, calls=%fused_computation.11.clone.1 | convolution fusion | flops 342622208 | bytes 8077316 | tf_op jit(solution)/shard_map/while/body/eval_jaxpr/hqk,khd->qhd/dot_general | solution.py:57
  43.5 0.0 copy-start.2
  43.5 0.9 copy-done.2
  44.5 0.6 dynamic_slice.32
  45.0 0.7 add_select_fusion.2
  45.7 0.3 fusion.44
  46.0 0.1 bitcast_compare_fusion.2
  46.1 0.5 copy.44
  46.6 0.1 broadcast_in_dim.107
  46.7 0.4 copy.45
  47.1 0.0 copy-start
  47.1 0.0 copy-start.1
  47.1 2.7 %fusion.45 = (f32[4,512]{1,0:T(4,128)S(1)}, f32[4,512,640]{2,1,0:T(8,128)S(1)}) fusion(pred[512,640]{1,0:T(8,128)(4,1)S(1)} %copy.44, bf16[640,4,256]{2,0,1:T(8,128)(2,1)} %get-tuple-element.236, bf16[2,512,4,128]{3,1,0,2:T(8,128)(2,1)} %get-tuple-element.235, s32[]{:T(128)S(6)} %copy.51), kind=kOutput, calls=%fused_computation.3.clone.1 | convolution fusion | flops 339474432 | bytes 6758404 | tf_op jit(solution)/shard_map/while/body/eval_jaxpr/qhd,khd->hqk/dot_general | solution.py:45
  49.8 1.8 %fusion.46 = f32[4,512]{1,0:T(4,128)S(1)} fusion(f32[4,512,640]{2,1,0:T(8,128)S(1)} %get-tuple-element.212, f32[512,640]{1,0:T(8,128)S(1)} %copy.45, f32[4,512]{1,0:T(4,128)S(1)} %get-tuple-element.213, pred[512,640]{1,0:T(8,128)(4,1)S(1)} %copy.44), kind=kLoop, calls=%fused_computation.4.clone.1 | loop fusion | flops 6551552 | bytes 6897664 | tf_op jit(solution)/shard_map/while/body/eval_jaxpr/reduce_sum | solution.py:56
  51.6 0.0 copy-done
  51.6 0.0 copy-done.1
  51.7 2.4 %fusion.47 = bf16[2,512,4,128]{3,1,0,2:T(8,128)(2,1)S(1)} fusion(bf16[2,512,4,128]{3,1,0,2:T(8,128)(2,1)S(1)} %copy-done.1, s32[]{:T(128)S(6)} %copy.51, f32[4,512,640]{2,1,0:T(8,128)S(1)} %get-tuple-element.212, f32[512,640]{1,0:T(8,128)S(1)} %copy.45, f32[4,512]{1,0:T(4,128)S(1)} %get-tuple-element.213, pred[512,640]{1,0:T(8,128)(4,1)S(1)} %copy.44, ...), kind=kOutput, calls=%fused_computation.11.clone.1 | convolution fusion | flops 342622208 | bytes 8077316 | tf_op jit(solution)/shard_map/while/body/eval_jaxpr/hqk,khd->qhd/dot_general | solution.py:57
  54.1 0.0 copy-start.2
  54.1 0.9 copy-done.2
  55.1 27.5 %pmax.7 = f32[1024,4]{0,1:T(4,128)S(1)} all-reduce(f32[1024,4]{0,1:T(4,128)S(1)} %bitcast.72), channel_id=1, replica_groups=mesh['frame'=4,'space'=8] {'space'}, use_global_device_ids=true, to_apply=%region_4.5 | all-reduce | flops 4096 | bytes 32768 | tf_op jit(solution)/shard_map/pmax | solution.py:70
  82.6 1.0 copy.35
  83.6 0.0 reduce-scatter.7.cloned.1.call-update
  83.6 0.0 reduce-scatter.5.cloned.1.call-start
  83.7 3.2 %convert_multiply_fusion = f32[1024,4,128]{2,0,1:T(8,128)} fusion(bf16[2,512,4,128]{3,1,0,2:T(8,128)(2,1)} %get-tuple-element.108, f32[1024,4]{0,1:T(4,128)S(1)} %subtract_exponential_fusion), kind=kLoop, calls=%fused_computation.36 | loop fusion | flops 1048576 | bytes 3162112 | tf_op jit(solution)/shard_map/mul | solution.py:72
  86.8 0.0 reduce-scatter.5.cloned.1.call-update
  86.8 26.0 %reduce-scatter.7.cloned.1.call-done = f32[128,4]{1,0:T(8,128)} async-done(((f32[1024,4]{1,0:T(8,128)}), f32[128,4]{1,0:T(8,128)}) %reduce-scatter.7.cloned.1.call-update) | async-done | bytes 2064
  112.9 0.9 copy.36
  113.8 35.4 %reduce-scatter.5.cloned.1.call-done = f32[128,4,128]{2,0,1:T(8,128)} async-done(((f32[1024,4,128]{2,0,1:T(8,128)}), f32[128,4,128]{2,0,1:T(8,128)}) %reduce-scatter.5.cloned.1.call-update) | async-done | bytes 262160 | tf_op jit(solution)/shard_map/reduce_scatter | solution.py:74
  149.2 1.1 divide_convert_fusion.1
  150.3 0.1 copy.33
  150.4 0.8 copy.34
  (13 shorter events, 0.1 us)
Async XLA Ops:
  6.5 9.5 %slice-start = ((bf16[128,4,384]{2,1,0:T(4,128)(2,1)}), bf16[128,4,256]{2,1,0:T(4,128)(2,1)S(1)}, s32[]{:S(2)}) async-start(bf16[128,4,384]{2,1,0:T(4,128)(2,1)} %param.7), calls=%async_computation.6 | async-start | bytes 524288 | tf_op jit(solution)/shard_map/slice | solution.py:25
  6.5 9.5 %copy-start.3 = (s32[8,8]{1,0:T(8,128)S(1)}, s32[8,8]{1,0:T(8,128)}, u32[]{:S(2)}) copy-start(s32[8,8]{1,0:T(8,128)} %param.11) | copy-start | bytes 772
  6.5 9.7 %copy-start.5 = (s32[8]{0:T(128)S(1)}, s32[8]{0:T(128)}, u32[]{:S(2)}) copy-start(s32[8]{0:T(128)} %param.10) | copy-start | bytes 100
  6.5 9.7 %copy-start.4 = (s32[4]{0:T(128)S(1)}, s32[4]{0:T(128)}, u32[]{:S(2)}) copy-start(s32[4]{0:T(128)} %param.9) | copy-start | bytes 52
  6.5 27.3 %all-gather.2.cloned.1.call-start = ((), (), s32[]{:S(2)}) async-start(), calls=%async_computation.3 | async-start | bytes 1179648 | tf_op jit(solution)/shard_map/all_gather | solution.py:30
  10.8 18.8 %all-to-all-start = ((bf16[1,128,16,256]{3,1,0,2:T(8,128)(2,1)}), bf16[1,128,16,256]{3,1,0,2:T(8,128)(2,1)S(1)}, u32[]{:S(2)}, u32[]{:S(2)}) async-start(bf16[1,128,16,256]{3,1,0,2:T(8,128)(2,1)} %copy.28), calls=%async_computation | async-start | bytes 2097152 | tf_op jit(solution)/shard_map/all_to_all | solution.py:20
  16.0 96.9 %reduce-scatter.7.cloned.1.call-start = ((), (), s32[]{:S(2)}) async-start(), calls=%async_computation.5 | async-start | bytes 589824
  36.5 4.5 %copy-start = (bf16[640,4,256]{2,0,1:T(8,128)(2,1)S(1)}, bf16[640,4,256]{2,0,1:T(8,128)(2,1)}, u32[]{:S(2)}) copy-start(bf16[640,4,256]{2,0,1:T(8,128)(2,1)} %get-tuple-element.236) | copy-start | bytes 3932164 | tf_op jit(solution)/shard_map/while
  36.5 4.5 %copy-start.1 = (bf16[2,512,4,128]{3,1,0,2:T(8,128)(2,1)S(1)}, bf16[2,512,4,128]{3,1,0,2:T(8,128)(2,1)}, u32[]{:S(2)}) copy-start(bf16[2,512,4,128]{3,1,0,2:T(8,128)(2,1)} %get-tuple-element.223) | copy-start | bytes 3145732 | tf_op jit(solution)/shard_map/while
  43.5 1.0 copy-start.2
  47.1 4.5 %copy-start = (bf16[640,4,256]{2,0,1:T(8,128)(2,1)S(1)}, bf16[640,4,256]{2,0,1:T(8,128)(2,1)}, u32[]{:S(2)}) copy-start(bf16[640,4,256]{2,0,1:T(8,128)(2,1)} %get-tuple-element.236) | copy-start | bytes 3932164 | tf_op jit(solution)/shard_map/while
  47.1 4.5 %copy-start.1 = (bf16[2,512,4,128]{3,1,0,2:T(8,128)(2,1)S(1)}, bf16[2,512,4,128]{3,1,0,2:T(8,128)(2,1)}, u32[]{:S(2)}) copy-start(bf16[2,512,4,128]{3,1,0,2:T(8,128)(2,1)} %get-tuple-element.223) | copy-start | bytes 3145732 | tf_op jit(solution)/shard_map/while
  54.1 1.0 copy-start.2
  83.6 65.6 %reduce-scatter.5.cloned.1.call-start = ((), (), s32[]{:S(2)}) async-start(), calls=%async_computation.4 | async-start | bytes 2359296 | tf_op jit(solution)/shard_map/reduce_scatter | solution.py:74
Sparse Core Ops, SparseCore 0:
  9.0 24.8 all-gather.1
  83.7 29.0 reduce-scatter.6
  115.3 33.8 reduce-scatter.4
where the time goes:
time: 158 us
  waiting for transfers between devices  77.7 us (49%)
  blocking collectives  27.5 us (17%)
  between operations  13.2 us (8%)
  local copies, waits for them, and re-layouts  12.3 us (8%)
  other arithmetic  10.9 us (7%)
  matrix products  10.8 us (7%)
  starting transfers between devices  5.24 us (3%)
    reduce_scatter x1, waiting for transfers between devices, body(): lax.psum_scatter(scaled, 'space', scatter_dimension=0, tiled=True)  35.4 us
    pmax x1, blocking collectives, body(): overall = lax.pmax(lse, 'space')  27.5 us
    unnamed x4, waiting for transfers between devices  26.1 us
    all_to_all x1, waiting for transfers between devices, body(): lax.all_to_all(past_cache, 'frame', split_axis=2, concat_axis=0, tiled=True)  13.2 us
    dot_general x2, matrix products, one_block(): jnp.einsum('qhd,khd->hqk', queries, key_sets[..., :head_size], preferred_...  5.38 us
    unnamed x11, local copies, waits for them, and re-layouts  5.18 us
    all_to_all x1, starting transfers between devices, body(): lax.all_to_all(past_cache, 'frame', split_axis=2, concat_axis=0, tiled=True)  5.16 us
    dot_general x2, matrix products, one_block(): jnp.einsum('hqk,khd->qhd', weights.astype(jnp.bfloat16), key_sets[..., he...  4.86 us
  transfers between devices with their start and end apart: 4, of which 4 were waited for; matrix products, arithmetic and copies ran while one was open for 5% of the time, Pallas kernels for 0%

commit v1 on v0

v1 whole, which is shorter than its diff:
```python
import functools
import math

import jax
import jax.numpy as jnp
from jax import lax
from jax.experimental import pallas as pl
from jax.experimental.pallas import tpu as pltpu
from jax.sharding import PartitionSpec as P

HIDDEN = -1e30
FLOOR = -1e29
MESH = pl.DeviceIdType.MESH
LOG2E = math.log2(math.e)


def attend(
    frames,
    members,
    heads,
    rank_ref,
    depth_ref,
    lists_ref,
    past_ref,
    qkv_ref,
    out_ref,
    kv,
    queries,
    values,
    share_out,
    share_in,
    lse_out,
    lse_in,
    local_sem,
    past_send,
    past_recv,
    fwd_send,
    fwd_recv,
    query_send,
    query_recv,
    share_send,
    share_recv,
    lse_send,
    lse_recv,
):
    toks = past_ref.shape[1]
    dim = past_ref.shape[2] // 2
    scale = LOG2E / math.sqrt(dim)
    fi = lax.axis_index("frame")
    si = lax.axis_index("space")
    group = si // 2
    core = si % 2
    peer = (fi, group * 2 + 1 - core)

    def frame_at(slot):
        return lax.rem(fi + slot, frames)

    def tile_at(slot):
        return lax.rem(group + slot, members) * 2 + core

    local = [
        [
            pltpu.make_async_copy(past_ref.at[fi * heads + h], kv.at[0, h, 0], local_sem.at[h, 0]),
            pltpu.make_async_copy(
                qkv_ref.at[h, :, pl.ds(dim, 2 * dim)], kv.at[0, h, frames], local_sem.at[h, 1]
            ),
            pltpu.make_async_copy(
                qkv_ref.at[h, :, pl.ds(0, dim)], queries.at[h, 0], local_sem.at[h, 2]
            ),
        ]
        for h in range(heads)
    ]
    for copies in local:
        for copy in copies:
            copy.start()

    def remote(src, dst, send_sem, recv_sem, device):
        return pltpu.make_async_remote_copy(
            src_ref=src,
            dst_ref=dst,
            send_sem=send_sem,
            recv_sem=recv_sem,
            device_id=device,
            device_id_type=MESH,
        )

    past_in = {}
    query_in = {}
    forward = {}
    for h in range(heads):
        for j in range(1, frames):
            to = frame_at(frames - j)
            past_in[h, j] = remote(
                past_ref.at[to * heads + h],
                kv.at[0, h, j],
                past_send.at[h, j],
                past_recv.at[h, j],
                (to, si),
            )
        for j in range(1, members):
            query_in[h, j] = remote(
                qkv_ref.at[h, :, pl.ds(0, dim)],
                queries.at[h, j],
                query_send.at[h, j],
                query_recv.at[h, j],
                (fi, tile_at(members - j)),
            )
        for j in range(frames + 1):
            if j == 0:
                src = past_ref.at[fi * heads + h]
            elif j == frames:
                src = qkv_ref.at[h, :, pl.ds(dim, 2 * dim)]
            else:
                src = kv.at[0, h, j]
            forward[h, j] = remote(
                src, kv.at[1, h, j], fwd_send.at[h, j], fwd_recv.at[h, j], peer
            )

    barrier = pltpu.get_barrier_semaphore()
    partners = [(frame_at(j), si) for j in range(1, frames)]
    partners += [(fi, tile_at(j)) for j in range(1, members)]
    partners.append(peer)
    for partner in partners:
        pl.semaphore_signal(barrier, inc=1, device_id=partner, device_id_type=MESH)
    pl.semaphore_wait(barrier, len(partners))

    for h in range(heads):
        for j in range(1, frames):
            past_in[h, j].start()
        for j in range(1, members):
            query_in[h, j].start()
        forward[h, 0].start()
        forward[h, frames].start()

    lse_out[...] = jnp.zeros_like(lse_out)
    lse_in[0] = jnp.zeros_like(lse_in[0])

    def pass_on(h):
        for j in range(1, frames):
            past_in[h, j].wait_recv()
            forward[h, j].start()

    def bias_of(key_tile, slot, tile):
        sees = lists_ref[tile, key_tile] > 0
        if slot < frames:
            sees = jnp.logical_and(
                sees, rank_ref[frame_at(slot)] >= frames - depth_ref[tile]
            )
        return jnp.where(sees, 0.0, HIDDEN)

    key_tiles = (si, group * 2 + 1 - core)
    span = (frames + 1) * toks
    lanes = lax.broadcasted_iota(jnp.int32, (1, 2 * toks), 1)
    share_copies = {}

    def compute(h, pair):
        slots = (2 * pair, 2 * pair + 1)
        query = queries[h, slots[0] : slots[0] + 2].reshape(2 * toks, dim)
        tiles = [tile_at(j) for j in slots]
        scores = []
        biases = []
        peak = jnp.full((1, 2 * toks), FLOOR, jnp.float32)
        for side in range(2):
            keys = kv[side, h, :, :, :dim].reshape(span, dim)
            score = lax.dot_general(
                keys, query, (((1,), (1,)), ((), ())), preferred_element_type=jnp.float32
            )
            scores.append(score)
            for slot in range(frames + 1):
                bias = jnp.where(
                    lanes < toks,
                    bias_of(key_tiles[side], slot, tiles[0]),
                    bias_of(key_tiles[side], slot, tiles[1]),
                )
                biases.append(bias)
                block = score[slot * toks : (slot + 1) * toks]
                peak = jnp.maximum(peak, jnp.max(block, axis=0, keepdims=True) * scale + bias)
        total = jnp.zeros((1, 2 * toks), jnp.float32)
        weighted = jnp.zeros((dim, 2 * toks), jnp.float32)
        for side in range(2):
            weights = []
            for slot in range(frames + 1):
                block = scores[side][slot * toks : (slot + 1) * toks]
                shift = peak - biases[side * (frames + 1) + slot]
                weight = jnp.exp2(block * scale - shift)
                total += jnp.sum(weight, axis=0, keepdims=True)
                weights.append(weight.astype(jnp.bfloat16))
            weighted += jnp.dot(
                values[h % 2, side],
                jnp.concatenate(weights, 0),
                preferred_element_type=jnp.float32,
            )
        safe = jnp.maximum(total, 1.0)
        share = (weighted * (1.0 / safe)).astype(jnp.bfloat16)
        lse = peak + jnp.log(safe) * LOG2E
        for at, j in enumerate(slots):
            part = share[:, at * toks : (at + 1) * toks]
            lse_part = lse[:, at * toks : (at + 1) * toks]
            if j == 0:
                share_in[h, 0] = part
                lse_in[0, h : h + 1, :] = lse_part
            else:
                share_out[h, j] = part
                lse_out[j, h : h + 1, :] = lse_part
                back = members - j
                copy = remote(
                    share_out.at[h, j],
                    share_in.at[h, back],
                    share_send.at[h, back],
                    share_recv.at[h, back],
                    (fi, tile_at(j)),
                )
                copy.start()
                share_copies[h, back] = copy

    pass_on(0)
    for h in range(heads):
        for copy in local[h]:
            copy.wait()
        for j in range(frames + 1):
            forward[h, j].wait_recv()
        for side in range(2):
            for slot in range(frames + 1):
                values[h % 2, side, :, slot * toks : (slot + 1) * toks] = kv[
                    side, h, slot, :, dim:
                ].T
        for at, pair in enumerate(reversed(range(members // 2))):
            for j in (2 * pair, 2 * pair + 1):
                if j > 0:
                    query_in[h, j].wait_recv()
            compute(h, pair)
            if at == 0 and h + 1 < heads:
                pass_on(h + 1)

    lse_copies = {}
    for j in range(1, members):
        back = members - j
        lse_copies[back] = remote(
            lse_out.at[j], lse_in.at[back], lse_send.at[back], lse_recv.at[back], (fi, tile_at(j))
        )
        lse_copies[back].start()
    for j in range(1, members):
        lse_copies[j].wait_recv()
    for h in range(heads):
        for j in range(1, members):
            share_copies[h, j].wait_recv()
        rows = [lse_in[j, h : h + 1, :] for j in range(members)]
        top = functools.reduce(jnp.maximum, rows)
        factors = [jnp.exp2(row - top) for row in rows]
        denominator = functools.reduce(jnp.add, factors)
        summed = functools.reduce(
            jnp.add,
            [share_in[h, j].astype(jnp.float32) * factors[j] for j in range(members)],
        )
        out_ref[:, h * dim : (h + 1) * dim] = (summed / denominator).T.astype(out_ref.dtype)

    for copies in (past_in, query_in, forward, share_copies, lse_copies):
        for copy in copies.values():
            copy.wait_send()


def body(qkv_now, past_cache, frame_rank, frame_depth, tile_lists):
    toks, heads, width = qkv_now.shape
    dim = width // 3
    frames = lax.axis_size("frame")
    members = lax.axis_size("space") // 2
    past = jnp.transpose(past_cache[0], (1, 0, 2))
    qkv = jnp.transpose(qkv_now, (1, 0, 2))
    lse_rows = -(-heads // 8) * 8
    dma = pltpu.SemaphoreType.DMA
    smem = pl.BlockSpec(memory_space=pltpu.SMEM)
    return pl.pallas_call(
        functools.partial(attend, frames, members, heads),
        out_shape=jax.ShapeDtypeStruct((toks, heads * dim), jnp.bfloat16),
        in_specs=[smem, smem, smem] + [pl.BlockSpec(memory_space=pl.ANY)] * 2,
        out_specs=pl.BlockSpec(memory_space=pltpu.VMEM),
        scratch_shapes=[
            pltpu.VMEM((2, heads, frames + 1, toks, 2 * dim), jnp.bfloat16),
            pltpu.VMEM((heads, members, toks, dim), jnp.bfloat16),
            pltpu.VMEM((2, 2, dim, (frames + 1) * toks), jnp.bfloat16),
            pltpu.VMEM((heads, members, dim, toks), jnp.bfloat16),
            pltpu.VMEM((heads, members, dim, toks), jnp.bfloat16),
            pltpu.VMEM((members, lse_rows, toks), jnp.float32),
            pltpu.VMEM((members, lse_rows, toks), jnp.float32),
            dma((heads, 3)),
            dma((heads, frames)),
            dma((heads, frames)),
            dma((heads, frames + 1)),
            dma((heads, frames + 1)),
            dma((heads, members)),
            dma((heads, members)),
            dma((heads, members)),
            dma((heads, members)),
            dma((members,)),
            dma((members,)),
        ],
        compiler_params=pltpu.CompilerParams(
            collective_id=0, has_side_effects=True, vmem_limit_bytes=48 * 1024 * 1024
        ),
    )(frame_rank, frame_depth, tile_lists, past, qkv)


def solution(mesh):
    in_specs = (P("space", "frame", None), P("frame", "space", None, None), P(), P(), P())
    out_specs = P("space", "frame")
    return jax.shard_map(body, mesh=mesh, in_specs=in_specs, out_specs=out_specs, check_vma=False)
```

time: 158 us -> 36.8 us (0.23)
  waiting for transfers between devices: 77.7 us -> 0 us
  Pallas kernels: 0 us -> 32.7 us
  blocking collectives: 27.5 us -> 0 us
  between operations: 13.2 us -> 0.05 us
  other arithmetic: 10.9 us -> 0 us
  matrix products: 10.8 us -> 0 us
  local copies, waits for them, and re-layouts: 12.3 us -> 3.92 us
  starting transfers between devices: 5.24 us -> 0 us
    reduce_scatter x1 -> x0, waiting for transfers between devices: 35.4 us -> none  [body(): lax.psum_scatter(scaled, 'space', scatter_dimension=0, tiled=True)]
    pallas_call x0 -> x1, Pallas kernels: none -> 32.7 us  [body(): pl.pallas_call(functools.partial(attend, frames, members, heads), out_sha...]
    pmax x1 -> x0, blocking collectives: 27.5 us -> none  [body(): overall = lax.pmax(lse, 'space')]
    unnamed x4 -> x0, waiting for transfers between devices: 26.1 us -> none
    all_to_all x1 -> x0, waiting for transfers between devices: 13.2 us -> none  [body(): lax.all_to_all(past_cache, 'frame', split_axis=2, concat_axis=0, tiled=True)]
    dot_general x6 -> x0, matrix products: 10.8 us -> none  [the longest x2 5.38 us: one_block(): jnp.einsum('qhd,khd->hqk', queries, key_sets[..., :head_size], preferred_...]
    all_to_all x1 -> x0, starting transfers between devices: 5.16 us -> none  [body(): lax.all_to_all(past_cache, 'frame', split_axis=2, concat_axis=0, tiled=True)]
    reduce_sum x2 -> x0, other arithmetic: 3.59 us -> none  [one_block(): totals = jnp.sum(weights, axis=-1)]
  transfers between devices with their start and end apart: 4 -> 0, of which waited for: 4 -> 0; matrix products, arithmetic and copies ran while one was open for 5% -> 0% of each run, Pallas kernels for 0% -> 0%
where the time goes in v1:
time: 36.8 us; the launch traced here: 36.7 us
  Pallas kernels  32.7 us (89%)
  local copies, waits for them, and re-layouts  3.92 us (11%)
    pallas_call x1, Pallas kernels, body(): pl.pallas_call(functools.partial(attend, frames, members, heads), out_sha...  32.7 us
    unnamed x9, local copies, waits for them, and re-layouts  3.92 us

profile of v1, /device:TPU:0, one launch (start us, length us, event | category | flops | bytes accessed | tf_op | source)
XLA Modules:
  0.0 36.7 jit_solution(8856219096067646511)
XLA Ops:
  0.0 1.0 %copy.11 = bf16[128,4,384]{2,0,1:T(8,128)(2,1)S(1)} copy(bf16[128,4,384]{2,1,0:T(4,128)(2,1)} %param.5) | data formatting | bytes 786432 | tf_op args[0]
  1.0 0.0 copy-start
  1.1 1.6 %copy.10 = bf16[1,128,16,256]{3,1,2,0:T(8,128)(2,1)S(1)} copy(bf16[1,128,16,256]{3,2,1,0:T(8,128)(2,1)} %param.6) | data formatting | bytes 2097152 | tf_op args[1]
  2.6 0.0 copy-start.1
  2.6 0.0 copy-start.2
  2.7 0.0 copy-done
  2.7 0.6 %copy-done.1 = s32[4]{0:T(128)S(1)} copy-done((s32[4]{0:T(128)S(1)}, s32[4]{0:T(128)}, u32[]{:S(2)}) %copy-start.1) | copy-done | bytes 40
  3.3 0.0 copy-done.2
  3.3 32.7 %shard_map.55 = bf16[128,512]{1,0:T(8,128)(2,1)S(1)} custom-call(s32[4]{0:T(128)S(1)} %copy-done.1, s32[8]{0:T(128)S(1)} %copy-done.2, s32[8,8]{1,0:T(8,128)S(1)} %copy-done, bf16[16,128,256]{2,1,0:T(8,128)(2,1)S(1)} %bitcast.8, bf16[4,128,384]{2,1,0:T(8,128)(2,1)S(1)} %bitcast.9), custom_call_target="tpu_custom_call" | custom-call | tf_op jit(solution)/shard_map/pallas_call | solution.py:272
  36.0 0.7 %copy.13 = bf16[128,512]{1,0:T(8,128)(2,1)} copy(bf16[128,512]{1,0:T(8,128)(2,1)S(1)} %shard_map.55) | data formatting | bytes 262144
Async XLA Ops:
  1.0 1.6 %copy-start = (s32[8,8]{1,0:T(8,128)S(1)}, s32[8,8]{1,0:T(8,128)}, u32[]{:S(2)}) copy-start(s32[8,8]{1,0:T(8,128)} %lists_ref.1) | copy-start | bytes 772
  2.6 0.7 %copy-start.1 = (s32[4]{0:T(128)S(1)}, s32[4]{0:T(128)}, u32[]{:S(2)}) copy-start(s32[4]{0:T(128)} %rank_ref.1) | copy-start | bytes 52
  2.6 0.7 %copy-start.2 = (s32[8]{0:T(128)S(1)}, s32[8]{0:T(128)}, u32[]{:S(2)}) copy-start(s32[8]{0:T(128)} %depth_ref.1) | copy-start | bytes 100

commit v2 on v1

v2 whole, which is shorter than its diff:
```python
import functools
import math

import jax
import jax.numpy as jnp
from jax import lax
from jax.experimental import pallas as pl
from jax.experimental.pallas import tpu as pltpu
from jax.sharding import PartitionSpec as P

HIDDEN = -1e30
FLOOR = -1e29
MESH = pl.DeviceIdType.MESH
LOG2E = math.log2(math.e)


def attend(
    frames,
    members,
    heads,
    rank_ref,
    depth_ref,
    lists_ref,
    past_ref,
    qkv_ref,
    out_ref,
    kv,
    queries,
    values,
    near_out,
    near_in,
    far_out,
    relay_in,
    far_in,
    near_lse_out,
    near_lse_in,
    far_lse_out,
    relay_lse_in,
    far_lse_in,
    held,
    held_lse,
    local_sem,
    past_send,
    past_recv,
    fwd_send,
    fwd_recv,
    query_send,
    query_recv,
    near_sem,
    far_sem,
    relay_recv,
    far_recv,
):
    toks = past_ref.shape[1]
    dim = past_ref.shape[2] // 2
    scale = LOG2E / math.sqrt(dim)
    fi = lax.axis_index("frame")
    si = lax.axis_index("space")
    group = si // 2
    core = si % 2
    peer = (fi, group * 2 + 1 - core)
    size = members // 2
    half = group // size
    place = group - half * size
    other = 1 - half
    inward = 1 - 2 * half
    outermost = jnp.logical_or(group == 0, group == members - 1)
    innermost = jnp.logical_or(group == size - 1, group == size)
    passes = jnp.logical_or(group == 1, group == members - 2)
    end_from = jnp.where(group == 1, members - 1, 0)
    end_to = members - 1 - end_from

    def frame_at(slot):
        return lax.rem(fi + slot, frames)

    def device_of(member):
        return (fi, member * 2 + core)

    def remote(src, dst, send_sem, recv_sem, device):
        return pltpu.make_async_remote_copy(
            src_ref=src,
            dst_ref=dst,
            send_sem=send_sem,
            recv_sem=recv_sem,
            device_id=device,
            device_id_type=MESH,
        )

    local = [
        [
            pltpu.make_async_copy(past_ref.at[fi * heads + h], kv.at[0, h, 0], local_sem.at[h, 0]),
            pltpu.make_async_copy(
                qkv_ref.at[h, :, pl.ds(dim, 2 * dim)], kv.at[0, h, frames], local_sem.at[h, 1]
            ),
            pltpu.make_async_copy(
                qkv_ref.at[h, :, pl.ds(0, dim)], queries.at[h, group], local_sem.at[h, 2]
            ),
        ]
        for h in range(heads)
    ]
    for copies in local:
        for copy in copies:
            copy.start()

    past_in = {}
    forward = {}
    query_out = {}
    query_on = {}
    for h in range(heads):
        for j in range(1, frames):
            to = frame_at(frames - j)
            past_in[h, j] = remote(
                past_ref.at[to * heads + h],
                kv.at[0, h, j],
                past_send.at[h, j],
                past_recv.at[h, j],
                (to, si),
            )
        for j in range(1, members):
            to = lax.rem(group + j, members)
            query_out[h, j] = (
                jnp.abs(to - group) != members - 1,
                remote(
                    qkv_ref.at[h, :, pl.ds(0, dim)],
                    queries.at[h, group],
                    query_send.at[h, j],
                    query_recv.at[h, group],
                    device_of(to),
                ),
            )
        query_on[h] = remote(
            queries.at[h, end_from],
            queries.at[h, end_from],
            query_send.at[h, 0],
            query_recv.at[h, end_from],
            device_of(end_to),
        )
        for j in range(frames + 1):
            if j == 0:
                src = past_ref.at[fi * heads + h]
            elif j == frames:
                src = qkv_ref.at[h, :, pl.ds(dim, 2 * dim)]
            else:
                src = kv.at[0, h, j]
            forward[h, j] = remote(
                src, kv.at[1, h, j], fwd_send.at[h, j], fwd_recv.at[h, j], peer
            )

    def query_wait(h, member):
        remote(
            queries.at[h, member],
            queries.at[h, member],
            query_send.at[h, 0],
            query_recv.at[h, member],
            peer,
        ).wait_recv()

    barrier = pltpu.get_barrier_semaphore()
    partners = [(frame_at(j), si) for j in range(1, frames)]
    partners += [device_of(lax.rem(group + j, members)) for j in range(1, members)]
    partners.append(peer)
    for partner in partners:
        pl.semaphore_signal(barrier, inc=1, device_id=partner, device_id_type=MESH)
    pl.semaphore_wait(barrier, len(partners))

    for h in range(heads):
        for j in range(1, frames):
            past_in[h, j].start()
        for j in range(1, members):
            pl.when(query_out[h, j][0])(query_out[h, j][1].start)
        forward[h, 0].start()
        forward[h, frames].start()

    near_lse_out[...] = jnp.zeros_like(near_lse_out)
    far_lse_out[...] = jnp.zeros_like(far_lse_out)

    def pass_on(h):
        @pl.when(passes)
        def _():
            query_wait(h, end_from)
            query_on[h].start()

        for j in range(1, frames):
            past_in[h, j].wait_recv()
            forward[h, j].start()

    def bias_of(key_tile, slot, tile):
        sees = lists_ref[tile, key_tile] > 0
        if slot < frames:
            sees = jnp.logical_and(
                sees, rank_ref[frame_at(slot)] >= frames - depth_ref[tile]
            )
        return jnp.where(sees, 0.0, HIDDEN)

    key_tiles = (si, group * 2 + 1 - core)
    span = (frames + 1) * toks
    lanes = lax.broadcasted_iota(jnp.int32, (1, 2 * toks), 1)

    def compute(h, first):
        query = queries[h, pl.ds(first, 2)].reshape(2 * toks, dim)
        tiles = [(first + at) * 2 + core for at in range(2)]
        scores = []
        biases = []
        peak = jnp.full((1, 2 * toks), FLOOR, jnp.float32)
        for side in range(2):
            keys = kv[side, h, :, :, :dim].reshape(span, dim)
            score = lax.dot_general(
                keys, query, (((1,), (1,)), ((), ())), preferred_element_type=jnp.float32
            )
            scores.append(score)
            for slot in range(frames + 1):
                bias = jnp.where(
                    lanes < toks,
                    bias_of(key_tiles[side], slot, tiles[0]),
                    bias_of(key_tiles[side], slot, tiles[1]),
                )
                biases.append(bias)
                block = score[slot * toks : (slot + 1) * toks]
                peak = jnp.maximum(peak, jnp.max(block, axis=0, keepdims=True) * scale + bias)
        total = jnp.zeros((1, 2 * toks), jnp.float32)
        weighted = jnp.zeros((dim, 2 * toks), jnp.float32)
        for side in range(2):
            weights = []
            for slot in range(frames + 1):
                block = scores[side][slot * toks : (slot + 1) * toks]
                shift = peak - biases[side * (frames + 1) + slot]
                weight = jnp.exp2(block * scale - shift)
                total += jnp.sum(weight, axis=0, keepdims=True)
                weights.append(weight.astype(jnp.bfloat16))
            weighted += jnp.dot(
                values[h % 2, side],
                jnp.concatenate(weights, 0),
                preferred_element_type=jnp.float32,
            )
        safe = jnp.maximum(total, 1.0)
        share = weighted * (1.0 / safe)
        lse = peak + jnp.log(safe) * LOG2E
        return [
            (share[:, at * toks : (at + 1) * toks], lse[:, at * toks : (at + 1) * toks])
            for at in range(2)
        ]

    def far_copies(h):
        inner = []
        across = []
        beside = device_of(jnp.clip(group + inward, 0, members - 1))
        for i in range(size):
            dest = device_of(other * size + i)
            src = far_out.at[h, i]
            inner.append(remote(src, relay_in.at[h, i], far_sem.at[h, i], relay_recv.at[h, i], beside))
            across.append(remote(src, far_in.at[h], far_sem.at[h, i], far_recv.at[h, 0], dest))
            across.append(
                remote(
                    far_lse_out.at[h],
                    far_lse_in.at[h],
                    far_sem.at[h, size + i],
                    far_recv.at[h, 1],
                    dest,
                )
            )
        inner.append(
            remote(
                far_lse_out.at[h],
                relay_lse_in.at[h],
                far_sem.at[h, size],
                relay_recv.at[h, size],
                beside,
            )
        )
        return inner, across

    def send_far(h):
        inner, across = far_copies(h)

        @pl.when(jnp.logical_not(innermost))
        def _():
            for copy in inner:
                copy.start()

        @pl.when(innermost)
        def _():
            for copy in across:
                copy.start()

    def merge(h):
        for copy in far_copies(h)[0]:
            copy.wait_recv()
        for i in range(size):
            own = held_lse[i : i + 1, :]
            theirs = relay_lse_in[h, i : i + 1, :]
            top = jnp.maximum(own, theirs)
            own_factor = jnp.exp2(own - top)
            their_factor = jnp.exp2(theirs - top)
            both = own_factor + their_factor
            inverse = 1.0 / both
            far_out[h, i] = (
                held[i] * (own_factor * inverse)
                + relay_in[h, i].astype(jnp.float32) * (their_factor * inverse)
            ).astype(jnp.bfloat16)
            far_lse_out[h, i : i + 1, :] = top + jnp.log(both) * LOG2E
        send_far(h)

    def near_copies(h):
        copies = []
        for d in range(1, size):
            to = lax.rem(place + d, size)
            dest = device_of(half * size + to)
            copies.append(
                remote(
                    near_out.at[h, to],
                    near_in.at[h, size - d],
                    near_sem.at[h, 0, d],
                    near_sem.at[h, 1, size - d],
                    dest,
                )
            )
            copies.append(
                remote(
                    near_lse_out.at[h],
                    near_lse_in.at[h, size - d],
                    near_sem.at[h, 2, d],
                    near_sem.at[h, 3, size - d],
                    dest,
                )
            )
        return copies

    def finish(h):
        for copy in near_copies(h):
            copy.wait_recv()
        far_copies(h)[1][0].wait_recv()
        far_copies(h)[1][1].wait_recv()
        mine = pl.ds(place, 1)
        rows = [near_lse_out[h, mine, :], far_lse_in[h, mine, :]]
        parts = [near_out[h, place], far_in[h]]
        for d in range(1, size):
            rows.append(near_lse_in[h, d, mine, :])
            parts.append(near_in[h, d])
        top = functools.reduce(jnp.maximum, rows)
        factors = [jnp.exp2(row - top) for row in rows]
        inverse = 1.0 / functools.reduce(jnp.add, factors)
        summed = functools.reduce(
            jnp.add,
            [
                part.astype(jnp.float32) * (factor * inverse)
                for part, factor in zip(parts, factors)
            ],
        )
        out_ref[:, h * dim : (h + 1) * dim] = summed.T.astype(out_ref.dtype)

    pass_on(0)
    for h in range(heads):
        for copy in local[h]:
            copy.wait()
        for j in range(frames + 1):
            forward[h, j].wait_recv()
        for side in range(2):
            for slot in range(frames + 1):
                values[h % 2, side, :, slot * toks : (slot + 1) * toks] = kv[
                    side, h, slot, :, dim:
                ].T
        for i in range(size):
            member = other * size + i
            pl.when(jnp.logical_not(jnp.logical_and(passes, member == end_from)))(
                functools.partial(query_wait, h, member)
            )
        for pair in range(size // 2):
            for at, (share, lse) in enumerate(compute(h, other * size + 2 * pair)):
                i = 2 * pair + at
                held[i] = share
                held_lse[i : i + 1, :] = lse

        @pl.when(outermost)
        def _():
            for i in range(size):
                far_out[h, i] = held[i].astype(jnp.bfloat16)
                far_lse_out[h, i : i + 1, :] = held_lse[i : i + 1, :]
            send_far(h)

        if h + 1 < heads:
            pass_on(h + 1)
        for d in range(1, size):
            query_wait(h, half * size + lax.rem(place + d, size))
        for pair in range(size // 2):
            for at, (share, lse) in enumerate(compute(h, half * size + 2 * pair)):
                i = 2 * pair + at
                near_out[h, i] = share.astype(jnp.bfloat16)
                near_lse_out[h, i : i + 1, :] = lse
        for copy in near_copies(h):
            copy.start()
        pl.when(jnp.logical_not(outermost))(functools.partial(merge, h))
        if h > 0:
            finish(h - 1)
    finish(heads - 1)

    for h in range(heads):
        for j in range(1, frames):
            past_in[h, j].wait_send()
        for j in range(1, members):
            pl.when(query_out[h, j][0])(query_out[h, j][1].wait_send)
        pl.when(passes)(query_on[h].wait_send)
        for j in range(frames + 1):
            forward[h, j].wait_send()
        for copy in near_copies(h):
            copy.wait_send()

        @pl.when(jnp.logical_not(innermost))
        def _():
            for copy in far_copies(h)[0]:
                copy.wait_send()

        @pl.when(innermost)
        def _():
            for copy in far_copies(h)[1]:
                copy.wait_send()


def body(qkv_now, past_cache, frame_rank, frame_depth, tile_lists):
    toks, heads, width = qkv_now.shape
    dim = width // 3
    frames = lax.axis_size("frame")
    members = lax.axis_size("space") // 2
    past = jnp.transpose(past_cache[0], (1, 0, 2))
    qkv = jnp.transpose(qkv_now, (1, 0, 2))
    size = members // 2
    lse_rows = -(-size // 8) * 8
    dma = pltpu.SemaphoreType.DMA
    smem = pl.BlockSpec(memory_space=pltpu.SMEM)
    return pl.pallas_call(
        functools.partial(attend, frames, members, heads),
        out_shape=jax.ShapeDtypeStruct((toks, heads * dim), jnp.bfloat16),
        in_specs=[smem, smem, smem] + [pl.BlockSpec(memory_space=pl.ANY)] * 2,
        out_specs=pl.BlockSpec(memory_space=pltpu.VMEM),
        scratch_shapes=[
            pltpu.VMEM((2, heads, frames + 1, toks, 2 * dim), jnp.bfloat16),
            pltpu.VMEM((heads, members, toks, dim), jnp.bfloat16),
            pltpu.VMEM((2, 2, dim, (frames + 1) * toks), jnp.bfloat16),
            pltpu.VMEM((heads, size, dim, toks), jnp.bfloat16),
            pltpu.VMEM((heads, size, dim, toks), jnp.bfloat16),
            pltpu.VMEM((heads, size, dim, toks), jnp.bfloat16),
            pltpu.VMEM((heads, size, dim, toks), jnp.bfloat16),
            pltpu.VMEM((heads, dim, toks), jnp.bfloat16),
            pltpu.VMEM((heads, lse_rows, toks), jnp.float32),
            pltpu.VMEM((heads, size, lse_rows, toks), jnp.float32),
            pltpu.VMEM((heads, lse_rows, toks), jnp.float32),
            pltpu.VMEM((heads, lse_rows, toks), jnp.float32),
            pltpu.VMEM((heads, lse_rows, toks), jnp.float32),
            pltpu.VMEM((size, dim, toks), jnp.float32),
            pltpu.VMEM((lse_rows, toks), jnp.float32),
            dma((heads, 3)),
            dma((heads, frames)),
            dma((heads, frames)),
            dma((heads, frames + 1)),
            dma((heads, frames + 1)),
            dma((heads, members)),
            dma((heads, members)),
            dma((heads, 4, size)),
            dma((heads, 2 * size)),
            dma((heads, size + 1)),
            dma((heads, 2)),
        ],
        compiler_params=pltpu.CompilerParams(
            collective_id=0, has_side_effects=True, vmem_limit_bytes=48 * 1024 * 1024
        ),
    )(frame_rank, frame_depth, tile_lists, past, qkv)


def solution(mesh):
    in_specs = (P("space", "frame", None), P("frame", "space", None, None), P(), P(), P())
    out_specs = P("space", "frame")
    return jax.shard_map(body, mesh=mesh, in_specs=in_specs, out_specs=out_specs, check_vma=False)
```

time: 36.8 us -> 39.8 us (1.082)
  Pallas kernels: 32.7 us -> 35.6 us
    pallas_call x1, Pallas kernels: 32.7 us -> 35.6 us  [body(): pl.pallas_call(functools.partial(attend, frames, members, heads), out_sha...]
where the time goes in v2:
time: 39.8 us; the launch traced here: 39.6 us
  Pallas kernels  35.6 us (89%)
  local copies, waits for them, and re-layouts  3.92 us (10%)
    pallas_call x1, Pallas kernels, body(): pl.pallas_call(functools.partial(attend, frames, members, heads), out_sha...  35.6 us
    unnamed x9, local copies, waits for them, and re-layouts  3.92 us

profile of v2, /device:TPU:0, one launch (start us, length us, event | category | flops | bytes accessed | tf_op | source)
XLA Modules:
  0.0 39.6 jit_solution(5373996918477292771)
XLA Ops:
  0.0 1.0 %copy.11 = bf16[128,4,384]{2,0,1:T(8,128)(2,1)S(1)} copy(bf16[128,4,384]{2,1,0:T(4,128)(2,1)} %param.5) | data formatting | bytes 786432 | tf_op args[0]
  1.0 0.0 copy-start
  1.1 1.6 %copy.10 = bf16[1,128,16,256]{3,1,2,0:T(8,128)(2,1)S(1)} copy(bf16[1,128,16,256]{3,2,1,0:T(8,128)(2,1)} %param.6) | data formatting | bytes 2097152 | tf_op args[1]
  2.6 0.0 copy-start.1
  2.6 0.0 copy-start.2
  2.7 0.0 copy-done
  2.7 0.6 %copy-done.1 = s32[4]{0:T(128)S(1)} copy-done((s32[4]{0:T(128)S(1)}, s32[4]{0:T(128)}, u32[]{:S(2)}) %copy-start.1) | copy-done | bytes 40
  3.3 0.0 copy-done.2
  3.3 35.6 %shard_map.55 = bf16[128,512]{1,0:T(8,128)(2,1)S(1)} custom-call(s32[4]{0:T(128)S(1)} %copy-done.1, s32[8]{0:T(128)S(1)} %copy-done.2, s32[8,8]{1,0:T(8,128)S(1)} %copy-done, bf16[16,128,256]{2,1,0:T(8,128)(2,1)S(1)} %bitcast.8, bf16[4,128,384]{2,1,0:T(8,128)(2,1)S(1)} %bitcast.9), custom_call_target="tpu_custom_call" | custom-call | tf_op jit(solution)/shard_map/pallas_call | solution.py:429
  38.9 0.7 %copy.13 = bf16[128,512]{1,0:T(8,128)(2,1)} copy(bf16[128,512]{1,0:T(8,128)(2,1)S(1)} %shard_map.55) | data formatting | bytes 262144
Async XLA Ops:
  1.0 1.6 %copy-start = (s32[8,8]{1,0:T(8,128)S(1)}, s32[8,8]{1,0:T(8,128)}, u32[]{:S(2)}) copy-start(s32[8,8]{1,0:T(8,128)} %lists_ref.1) | copy-start | bytes 772
  2.6 0.7 %copy-start.1 = (s32[4]{0:T(128)S(1)}, s32[4]{0:T(128)}, u32[]{:S(2)}) copy-start(s32[4]{0:T(128)} %rank_ref.1) | copy-start | bytes 52
  2.6 0.7 %copy-start.2 = (s32[8]{0:T(128)S(1)}, s32[8]{0:T(128)}, u32[]{:S(2)}) copy-start(s32[8]{0:T(128)} %depth_ref.1) | copy-start | bytes 100

commit v3 on v1

v3 whole, which is shorter than its diff:
```python
import functools
import math

import jax
import jax.numpy as jnp
from jax import lax
from jax.experimental import pallas as pl
from jax.experimental.pallas import tpu as pltpu
from jax.sharding import PartitionSpec as P

HIDDEN = -1e30
FLOOR = -1e29
MESH = pl.DeviceIdType.MESH
LOG2E = math.log2(math.e)


def attend(
    frames,
    members,
    heads,
    rank_ref,
    depth_ref,
    lists_ref,
    past_ref,
    qkv_ref,
    out_ref,
    early_kv,
    late_kv,
    queries,
    early_values,
    late_values,
    bias_rows,
    part_sum,
    part_stat,
    share_out,
    share_in,
    lse_out,
    lse_in,
    local_sem,
    past_send,
    past_recv,
    fwd_send,
    fwd_recv,
    query_send,
    query_recv,
    share_send,
    share_recv,
    lse_send,
    lse_recv,
):
    toks = past_ref.shape[1]
    dim = past_ref.shape[2] // 2
    scale = LOG2E / math.sqrt(dim)
    fi = lax.axis_index("frame")
    si = lax.axis_index("space")
    group = si // 2
    core = si % 2
    beside = group * 2 + 1 - core
    peer = (fi, beside)
    size = members // 2
    half = group // size
    place = group - half * size
    passes = jnp.logical_or(group == 1, group == members - 2)
    end_from = jnp.where(group == 1, members - 1, 0)
    end_to = members - 1 - end_from

    def frame_at(slot):
        return lax.rem(fi + slot, frames)

    def device_of(member):
        return (fi, member * 2 + core)

    def remote(src, dst, send_sem, recv_sem, device):
        return pltpu.make_async_remote_copy(
            src_ref=src,
            dst_ref=dst,
            send_sem=send_sem,
            recv_sem=recv_sem,
            device_id=device,
            device_id_type=MESH,
        )

    def own_past(h):
        return past_ref.at[fi * heads + h]

    def own_now(h):
        return qkv_ref.at[h, :, pl.ds(dim, 2 * dim)]

    def own_query(h):
        return qkv_ref.at[h, :, pl.ds(0, dim)]

    local = [
        [
            pltpu.make_async_copy(own_past(h), early_kv.at[0, h, 0], local_sem.at[h, 0]),
            pltpu.make_async_copy(own_now(h), early_kv.at[0, h, 1], local_sem.at[h, 1]),
            pltpu.make_async_copy(own_query(h), queries.at[h, group], local_sem.at[h, 2]),
        ]
        for h in range(heads)
    ]
    for copies in local:
        for copy in copies:
            copy.start()

    def past_copy(h, j):
        to = frame_at(frames - j)
        return remote(
            past_ref.at[to * heads + h],
            late_kv.at[0, h, j - 1],
            past_send.at[h, j],
            past_recv.at[h, j],
            (to, si),
        )

    def early_forward(h, j):
        return remote(
            (own_past, own_now)[j](h),
            early_kv.at[1, h, j],
            fwd_send.at[h, frames - 1 + j],
            fwd_recv.at[h, frames - 1 + j],
            peer,
        )

    def late_forward(h, j):
        return remote(
            late_kv.at[0, h, j],
            late_kv.at[1, h, j],
            fwd_send.at[h, j],
            fwd_recv.at[h, j],
            peer,
        )

    def query_copy(h, j):
        to = lax.rem(group + j, members)
        return jnp.abs(to - group) != members - 1, remote(
            own_query(h),
            queries.at[h, group],
            query_send.at[h, j],
            query_recv.at[h, group],
            device_of(to),
        )

    def query_on(h):
        return remote(
            queries.at[h, end_from],
            queries.at[h, end_from],
            query_send.at[h, 0],
            query_recv.at[h, end_from],
            device_of(end_to),
        )

    def query_wait(h, member):
        remote(
            queries.at[h, member],
            queries.at[h, member],
            query_send.at[h, 0],
            query_recv.at[h, member],
            peer,
        ).wait_recv()

    def start_past(h):
        for j in range(1, frames):
            past_copy(h, j).start()

    def start_query(h):
        for j in range(1, members):
            wanted, copy = query_copy(h, j)
            pl.when(wanted)(copy.start)

    barrier = pltpu.get_barrier_semaphore()
    partners = [(frame_at(j), si) for j in range(1, frames)]
    partners += [device_of(lax.rem(group + j, members)) for j in range(1, members)]
    partners.append(peer)
    for partner in partners:
        pl.semaphore_signal(barrier, inc=1, device_id=partner, device_id_type=MESH)
    pl.semaphore_wait(barrier, len(partners))

    ahead = min(2, heads)
    for h in range(ahead):
        start_past(h)
        start_query(h)
        for j in range(2):
            early_forward(h, j).start()
    for h in range(ahead, heads):
        for j in range(2):
            early_forward(h, j).start()

    lse_out[...] = jnp.zeros_like(lse_out)
    lanes = lax.broadcasted_iota(jnp.int32, (1, 2 * toks), 1)

    def bias_of(key_tile, slot, tile):
        sees = lists_ref[tile, key_tile] > 0
        if slot < frames:
            sees = jnp.logical_and(
                sees, rank_ref[frame_at(slot)] >= frames - depth_ref[tile]
            )
        return jnp.where(sees, 0.0, HIDDEN)

    late_slots = frames - 1
    blocks = [(side, slot) for side in range(2) for slot in (0, frames)]
    blocks += [(side, slot) for side in range(2) for slot in range(1, frames)]
    early_count = 4
    for pair in range(size):
        for at, (side, slot) in enumerate(blocks):
            low, high = (
                bias_of((si, beside)[side], slot, (2 * pair + k) * 2 + core) for k in range(2)
            )
            bias_rows[pair, at : at + 1, :] = jnp.where(lanes < toks, low, high)

    def weigh(keys, query, pair, first, count, peak):
        score = lax.dot_general(
            keys, query, (((1,), (1,)), ((), ())), preferred_element_type=jnp.float32
        )
        parts = [score[at * toks : (at + 1) * toks] for at in range(count)]
        bias = [bias_rows[pair, first + at : first + at + 1, :] for at in range(count)]
        for part, row in zip(parts, bias):
            peak = jnp.maximum(peak, jnp.max(part, axis=0, keepdims=True) * scale + row)
        total = jnp.zeros((1, 2 * toks), jnp.float32)
        weights = []
        for part, row in zip(parts, bias):
            weight = jnp.exp2(part * scale - (peak - row))
            total += jnp.sum(weight, axis=0, keepdims=True)
            weights.append(weight.astype(jnp.bfloat16))
        return peak, total, jnp.concatenate(weights, 0)

    def query_of(h, pair):
        return queries[h, pl.ds(2 * pair, 2)].reshape(2 * toks, dim)

    def early(h, pair):
        keys = early_kv[:, h, :, :, :dim].reshape(4 * toks, dim)
        floor = jnp.full((1, 2 * toks), FLOOR, jnp.float32)
        peak, total, weights = weigh(keys, query_of(h, pair), pair, 0, early_count, floor)
        part_sum[h, pair] = jnp.dot(early_values[...], weights, preferred_element_type=jnp.float32)
        part_stat[h, pair, 0:1, :] = peak
        part_stat[h, pair, 1:2, :] = total

    def share_copy(h, member):
        return remote(
            share_out.at[h, member],
            share_in.at[h, group],
            share_send.at[h, member],
            share_recv.at[h, group],
            device_of(member),
        )

    def late(h, pair):
        keys = late_kv[:, h, :, :, :dim].reshape(2 * late_slots * toks, dim)
        before = part_stat[h, pair, 0:1, :]
        peak, total, weights = weigh(
            keys, query_of(h, pair), pair, early_count, 2 * late_slots, before
        )
        factor = jnp.exp2(before - peak)
        safe = jnp.maximum(total + part_stat[h, pair, 1:2, :] * factor, 1.0)
        inverse = 1.0 / safe
        weighted = jnp.dot(late_values[...], weights, preferred_element_type=jnp.float32)
        share = (weighted * inverse + part_sum[h, pair] * (factor * inverse)).astype(jnp.bfloat16)
        lse = peak + jnp.log(safe) * LOG2E
        for at in range(2):
            member = 2 * pair + at
            share_out[h, member] = share[:, at * toks : (at + 1) * toks]
            lse_out[member, h : h + 1, :] = lse[:, at * toks : (at + 1) * toks]
            pl.when(member != group)(share_copy(h, member).start)

    def early_head(h):
        for copy in local[h]:
            copy.wait()
        for j in range(2):
            early_forward(h, j).wait_recv()
        for side in range(2):
            for j in range(2):
                at = (2 * side + j) * toks
                early_values[:, at : at + toks] = early_kv[side, h, j, :, dim:].T
        for d in range(1, size):
            query_wait(h, half * size + lax.rem(place + d, size))
        for k in range(size // 2):
            early(h, half * (size // 2) + k)

        @pl.when(passes)
        def _():
            query_wait(h, end_from)
            query_on(h).start()

        for i in range(size):
            member = (1 - half) * size + i
            pl.when(jnp.logical_not(jnp.logical_and(passes, member == end_from)))(
                functools.partial(query_wait, h, member)
            )
        if h + ahead < heads:
            start_query(h + ahead)
        for k in range(size // 2):
            early(h, (1 - half) * (size // 2) + k)

    def pass_on(h):
        for j in range(1, frames):
            past_copy(h, j).wait_recv()
            late_forward(h, j - 1).start()
        if h + ahead < heads:
            start_past(h + ahead)

    def late_head(h):
        for j in range(late_slots):
            late_forward(h, j).wait_recv()
        for side in range(2):
            for j in range(late_slots):
                at = (side * late_slots + j) * toks
                late_values[:, at : at + toks] = late_kv[side, h, j, :, dim:].T
        for part in (1 - half, half):
            for k in range(size // 2):
                late(h, part * (size // 2) + k)

    passed = 0
    for h in range(heads):
        early_head(h)
        if 1 <= h <= heads - 2:
            pass_on(passed)
            passed += 1
    for h in range(heads):
        while passed <= h:
            pass_on(passed)
            passed += 1
        late_head(h)
        if passed < heads:
            pass_on(passed)
            passed += 1

    def lse_copy(j):
        member = lax.rem(group + j, members)
        return remote(
            lse_out.at[member],
            lse_in.at[group],
            lse_send.at[member],
            lse_recv.at[group],
            device_of(member),
        )

    for j in range(1, members):
        lse_copy(j).start()

    def arrived(j):
        member = lax.rem(group + j, members)
        return member, remote(
            lse_out.at[member], lse_in.at[member], lse_send.at[member], lse_recv.at[member], peer
        )

    for j in range(1, members):
        arrived(j)[1].wait_recv()
    for h in range(heads):
        rows = [lse_out[group, h : h + 1, :]]
        parts = [share_out[h, group]]
        for j in range(1, members):
            member = lax.rem(group + j, members)
            remote(
                share_out.at[h, member],
                share_in.at[h, member],
                share_send.at[h, member],
                share_recv.at[h, member],
                peer,
            ).wait_recv()
            rows.append(lse_in[member, h : h + 1, :])
            parts.append(share_in[h, member])
        top = functools.reduce(jnp.maximum, rows)
        factors = [jnp.exp2(row - top) for row in rows]
        inverse = 1.0 / functools.reduce(jnp.add, factors)
        summed = functools.reduce(
            jnp.add,
            [
                part.astype(jnp.float32) * (factor * inverse)
                for part, factor in zip(parts, factors)
            ],
        )
        out_ref[:, h * dim : (h + 1) * dim] = summed.T.astype(out_ref.dtype)

    for h in range(heads):
        for j in range(1, frames):
            past_copy(h, j).wait_send()
            late_forward(h, j - 1).wait_send()
        for j in range(2):
            early_forward(h, j).wait_send()
        for j in range(1, members):
            wanted, copy = query_copy(h, j)
            pl.when(wanted)(copy.wait_send)
            share_copy(h, lax.rem(group + j, members)).wait_send()
        pl.when(passes)(query_on(h).wait_send)
    for j in range(1, members):
        lse_copy(j).wait_send()


def body(qkv_now, past_cache, frame_rank, frame_depth, tile_lists):
    toks, heads, width = qkv_now.shape
    dim = width // 3
    frames = lax.axis_size("frame")
    members = lax.axis_size("space") // 2
    past = jnp.transpose(past_cache[0], (1, 0, 2))
    qkv = jnp.transpose(qkv_now, (1, 0, 2))
    lse_rows = -(-heads // 8) * 8
    bias_count = -(-2 * (frames + 1) // 8) * 8
    half = members // 2
    dma = pltpu.SemaphoreType.DMA
    smem = pl.BlockSpec(memory_space=pltpu.SMEM)
    return pl.pallas_call(
        functools.partial(attend, frames, members, heads),
        out_shape=jax.ShapeDtypeStruct((toks, heads * dim), jnp.bfloat16),
        in_specs=[smem, smem, smem] + [pl.BlockSpec(memory_space=pl.ANY)] * 2,
        out_specs=pl.BlockSpec(memory_space=pltpu.VMEM),
        scratch_shapes=[
            pltpu.VMEM((2, heads, 2, toks, 2 * dim), jnp.bfloat16),
            pltpu.VMEM((2, heads, frames - 1, toks, 2 * dim), jnp.bfloat16),
            pltpu.VMEM((heads, members, toks, dim), jnp.bfloat16),
            pltpu.VMEM((dim, 4 * toks), jnp.bfloat16),
            pltpu.VMEM((dim, 2 * (frames - 1) * toks), jnp.bfloat16),
            pltpu.VMEM((half, bias_count, 2 * toks), jnp.float32),
            pltpu.VMEM((heads, half, dim, 2 * toks), jnp.float32),
            pltpu.VMEM((heads, half, 8, 2 * toks), jnp.float32),
            pltpu.VMEM((heads, members, dim, toks), jnp.bfloat16),
            pltpu.VMEM((heads, members, dim, toks), jnp.bfloat16),
            pltpu.VMEM((members, lse_rows, toks), jnp.float32),
            pltpu.VMEM((members, lse_rows, toks), jnp.float32),
            dma((heads, 3)),
            dma((heads, frames)),
            dma((heads, frames)),
            dma((heads, frames + 1)),
            dma((heads, frames + 1)),
            dma((heads, members)),
            dma((heads, members)),
            dma((heads, members)),
            dma((heads, members)),
            dma((members,)),
            dma((members,)),
        ],
        compiler_params=pltpu.CompilerParams(
            collective_id=0, has_side_effects=True, vmem_limit_bytes=48 * 1024 * 1024
        ),
    )(frame_rank, frame_depth, tile_lists, past, qkv)


def solution(mesh):
    in_specs = (P("space", "frame", None), P("frame", "space", None, None), P(), P(), P())
    out_specs = P("space", "frame")
    return jax.shard_map(body, mesh=mesh, in_specs=in_specs, out_specs=out_specs, check_vma=False)
```

time: 36.8 us -> 40.4 us (1.098)
  Pallas kernels: 32.7 us -> 36.3 us
    pallas_call x1, Pallas kernels: 32.7 us -> 36.3 us  [body(): pl.pallas_call(functools.partial(attend, frames, members, heads), out_sha...]
where the time goes in v3:
time: 40.4 us; the launch traced here: 40.2 us
  Pallas kernels  36.3 us (90%)
  local copies, waits for them, and re-layouts  3.92 us (10%)
    pallas_call x1, Pallas kernels, body(): pl.pallas_call(functools.partial(attend, frames, members, heads), out_sha...  36.3 us
    unnamed x9, local copies, waits for them, and re-layouts  3.92 us

profile of v3, /device:TPU:0, one launch (start us, length us, event | category | flops | bytes accessed | tf_op | source)
XLA Modules:
  0.0 40.2 jit_solution(13402593738548227363)
XLA Ops:
  0.0 1.0 %copy.11 = bf16[128,4,384]{2,0,1:T(8,128)(2,1)S(1)} copy(bf16[128,4,384]{2,1,0:T(4,128)(2,1)} %param.5) | data formatting | bytes 786432 | tf_op args[0]
  1.0 0.0 copy-start
  1.1 1.6 %copy.10 = bf16[1,128,16,256]{3,1,2,0:T(8,128)(2,1)S(1)} copy(bf16[1,128,16,256]{3,2,1,0:T(8,128)(2,1)} %param.6) | data formatting | bytes 2097152 | tf_op args[1]
  2.6 0.0 copy-start.1
  2.6 0.0 copy-start.2
  2.7 0.0 copy-done
  2.7 0.6 %copy-done.1 = s32[4]{0:T(128)S(1)} copy-done((s32[4]{0:T(128)S(1)}, s32[4]{0:T(128)}, u32[]{:S(2)}) %copy-start.1) | copy-done | bytes 40
  3.3 0.0 copy-done.2
  3.3 36.3 %shard_map.55 = bf16[128,512]{1,0:T(8,128)(2,1)S(1)} custom-call(s32[4]{0:T(128)S(1)} %copy-done.1, s32[8]{0:T(128)S(1)} %copy-done.2, s32[8,8]{1,0:T(8,128)S(1)} %copy-done, bf16[16,128,256]{2,1,0:T(8,128)(2,1)S(1)} %bitcast.8, bf16[4,128,384]{2,1,0:T(8,128)(2,1)S(1)} %bitcast.9), custom_call_target="tpu_custom_call" | custom-call | tf_op jit(solution)/shard_map/pallas_call | solution.py:399
  39.6 0.7 %copy.13 = bf16[128,512]{1,0:T(8,128)(2,1)} copy(bf16[128,512]{1,0:T(8,128)(2,1)S(1)} %shard_map.55) | data formatting | bytes 262144
Async XLA Ops:
  1.0 1.6 %copy-start = (s32[8,8]{1,0:T(8,128)S(1)}, s32[8,8]{1,0:T(8,128)}, u32[]{:S(2)}) copy-start(s32[8,8]{1,0:T(8,128)} %lists_ref.1) | copy-start | bytes 772
  2.6 0.7 %copy-start.1 = (s32[4]{0:T(128)S(1)}, s32[4]{0:T(128)}, u32[]{:S(2)}) copy-start(s32[4]{0:T(128)} %rank_ref.1) | copy-start | bytes 52
  2.6 0.7 %copy-start.2 = (s32[8]{0:T(128)S(1)}, s32[8]{0:T(128)}, u32[]{:S(2)}) copy-start(s32[8]{0:T(128)} %depth_ref.1) | copy-start | bytes 100

commit v4 on v3

--- a/solution.py
+++ b/solution.py
@@ -89,17 +89,15 @@
     def own_query(h):
         return qkv_ref.at[h, :, pl.ds(0, dim)]
 
-    local = [
-        [
+    def local_copies(h):
+        return [
             pltpu.make_async_copy(own_past(h), early_kv.at[0, h, 0], local_sem.at[h, 0]),
             pltpu.make_async_copy(own_now(h), early_kv.at[0, h, 1], local_sem.at[h, 1]),
             pltpu.make_async_copy(own_query(h), queries.at[h, group], local_sem.at[h, 2]),
         ]
-        for h in range(heads)
-    ]
-    for copies in local:
-        for copy in copies:
-            copy.start()
+
+    def each(count, step):
+        lax.fori_loop(0, count, lambda at, carry: (step(at), carry)[1], 0)
 
     def past_copy(h, j):
         to = frame_at(frames - j)
@@ -174,16 +172,15 @@
         pl.semaphore_signal(barrier, inc=1, device_id=partner, device_id_type=MESH)
     pl.semaphore_wait(barrier, len(partners))
 
-    ahead = min(2, heads)
-    for h in range(ahead):
+    def start_head(h):
         start_past(h)
         start_query(h)
         for j in range(2):
             early_forward(h, j).start()
-    for h in range(ahead, heads):
-        for j in range(2):
-            early_forward(h, j).start()
-
+        for copy in local_copies(h):
+            copy.start()
+
+    each(heads, start_head)
     lse_out[...] = jnp.zeros_like(lse_out)
     lanes = lax.broadcasted_iota(jnp.int32, (1, 2 * toks), 1)
 
@@ -199,12 +196,15 @@
     blocks = [(side, slot) for side in range(2) for slot in (0, frames)]
     blocks += [(side, slot) for side in range(2) for slot in range(1, frames)]
     early_count = 4
-    for pair in range(size):
+
+    def set_bias(pair):
         for at, (side, slot) in enumerate(blocks):
             low, high = (
                 bias_of((si, beside)[side], slot, (2 * pair + k) * 2 + core) for k in range(2)
             )
             bias_rows[pair, at : at + 1, :] = jnp.where(lanes < toks, low, high)
+
+    each(size, set_bias)
 
     def weigh(keys, query, pair, first, count, peak):
         score = lax.dot_general(
@@ -257,11 +257,11 @@
         for at in range(2):
             member = 2 * pair + at
             share_out[h, member] = share[:, at * toks : (at + 1) * toks]
-            lse_out[member, h : h + 1, :] = lse[:, at * toks : (at + 1) * toks]
+            lse_out[member, pl.ds(h, 1), :] = lse[:, at * toks : (at + 1) * toks]
             pl.when(member != group)(share_copy(h, member).start)
 
     def early_head(h):
-        for copy in local[h]:
+        for copy in local_copies(h):
             copy.wait()
         for j in range(2):
             early_forward(h, j).wait_recv()
@@ -269,32 +269,25 @@
             for j in range(2):
                 at = (2 * side + j) * toks
                 early_values[:, at : at + toks] = early_kv[side, h, j, :, dim:].T
-        for d in range(1, size):
-            query_wait(h, half * size + lax.rem(place + d, size))
-        for k in range(size // 2):
-            early(h, half * (size // 2) + k)
-
-        @pl.when(passes)
-        def _():
-            query_wait(h, end_from)
-            query_on(h).start()
-
-        for i in range(size):
-            member = (1 - half) * size + i
-            pl.when(jnp.logical_not(jnp.logical_and(passes, member == end_from)))(
-                functools.partial(query_wait, h, member)
-            )
-        if h + ahead < heads:
-            start_query(h + ahead)
-        for k in range(size // 2):
-            early(h, (1 - half) * (size // 2) + k)
+
+        def step(k):
+            pair = lax.rem(half * (size // 2) + k, size)
+            for at in range(2):
+                member = 2 * pair + at
+                pl.when(member != group)(functools.partial(query_wait, h, member))
+
+                @pl.when(jnp.logical_and(passes, member == end_from))
+                def _():
+                    query_on(h).start()
+
+            early(h, pair)
+
+        each(size, step)
 
     def pass_on(h):
         for j in range(1, frames):
             past_copy(h, j).wait_recv()
             late_forward(h, j - 1).start()
-        if h + ahead < heads:
-            start_past(h + ahead)
 
     def late_head(h):
         for j in range(late_slots):
@@ -303,24 +296,19 @@
             for j in range(late_slots):
                 at = (side * late_slots + j) * toks
                 late_values[:, at : at + toks] = late_kv[side, h, j, :, dim:].T
-        for part in (1 - half, half):
-            for k in range(size // 2):
-                late(h, part * (size // 2) + k)
-
-    passed = 0
-    for h in range(heads):
-        early_head(h)
-        if 1 <= h <= heads - 2:
-            pass_on(passed)
-            passed += 1
-    for h in range(heads):
-        while passed <= h:
-            pass_on(passed)
-            passed += 1
-        late_head(h)
-        if passed < heads:
-            pass_on(passed)
-            passed += 1
+
+        def step(k):
+            late(h, lax.rem((1 - half) * (size // 2) + k, size))
+
+            @pl.when(jnp.logical_and(k == 0, h + 1 < heads))
+            def _():
+                pass_on(h + 1)
+
+        each(size, step)
+
+    each(heads, early_head)
+    pass_on(0)
+    each(heads, late_head)
 
     def lse_copy(j):
         member = lax.rem(group + j, members)
@@ -343,8 +331,9 @@
 
     for j in range(1, members):
         arrived(j)[1].wait_recv()
-    for h in range(heads):
-        rows = [lse_out[group, h : h + 1, :]]
+    def finish(h):
+        row = pl.ds(h, 1)
+        rows = [lse_out[group, row, :]]
         parts = [share_out[h, group]]
         for j in range(1, members):
             member = lax.rem(group + j, members)
@@ -355,7 +344,7 @@
                 share_recv.at[h, member],
                 peer,
             ).wait_recv()
-            rows.append(lse_in[member, h : h + 1, :])
+            rows.append(lse_in[member, row, :])
             parts.append(share_in[h, member])
         top = functools.reduce(jnp.maximum, rows)
         factors = [jnp.exp2(row - top) for row in rows]
@@ -367,9 +356,11 @@
                 for part, factor in zip(parts, factors)
             ],
         )
-        out_ref[:, h * dim : (h + 1) * dim] = summed.T.astype(out_ref.dtype)
-
-    for h in range(heads):
+        out_ref[:, pl.ds(pl.multiple_of(h * dim, dim), dim)] = summed.T.astype(out_ref.dtype)
+
+    each(heads, finish)
+
+    def sent(h):
         for j in range(1, frames):
             past_copy(h, j).wait_send()
             late_forward(h, j - 1).wait_send()
@@ -380,6 +371,8 @@
             pl.when(wanted)(copy.wait_send)
             share_copy(h, lax.rem(group + j, members)).wait_send()
         pl.when(passes)(query_on(h).wait_send)
+
+    each(heads, sent)
     for j in range(1, members):
         lse_copy(j).wait_send()
 

time: 40.4 us -> 38.5 us (0.953)
  Pallas kernels: 36.3 us -> 34.4 us
    pallas_call x1, Pallas kernels: 36.3 us -> 34.4 us  [body(): pl.pallas_call(functools.partial(attend, frames, members, heads), out_sha...]
where the time goes in v4:
time: 38.5 us; the launch traced here: 38.3 us
  Pallas kernels  34.4 us (89%)
  local copies, waits for them, and re-layouts  3.92 us (10%)
    pallas_call x1, Pallas kernels, body(): pl.pallas_call(functools.partial(attend, frames, members, heads), out_sha...  34.4 us
    unnamed x9, local copies, waits for them, and re-layouts  3.92 us

profile of v4, /device:TPU:0, one launch (start us, length us, event | category | flops | bytes accessed | tf_op | source)
XLA Modules:
  0.0 38.3 jit_solution(13779405758025559521)
XLA Ops:
  0.0 1.0 %copy.11 = bf16[128,4,384]{2,0,1:T(8,128)(2,1)S(1)} copy(bf16[128,4,384]{2,1,0:T(4,128)(2,1)} %param.5) | data formatting | bytes 786432 | tf_op args[0]
  1.0 0.0 copy-start
  1.1 1.6 %copy.10 = bf16[1,128,16,256]{3,1,2,0:T(8,128)(2,1)S(1)} copy(bf16[1,128,16,256]{3,2,1,0:T(8,128)(2,1)} %param.6) | data formatting | bytes 2097152 | tf_op args[1]
  2.6 0.0 copy-start.1
  2.6 0.0 copy-start.2
  2.7 0.0 copy-done
  2.7 0.6 %copy-done.1 = s32[4]{0:T(128)S(1)} copy-done((s32[4]{0:T(128)S(1)}, s32[4]{0:T(128)}, u32[]{:S(2)}) %copy-start.1) | copy-done | bytes 40
  3.3 0.0 copy-done.2
  3.3 34.4 %shard_map.55 = bf16[128,512]{1,0:T(8,128)(2,1)S(1)} custom-call(s32[4]{0:T(128)S(1)} %copy-done.1, s32[8]{0:T(128)S(1)} %copy-done.2, s32[8,8]{1,0:T(8,128)S(1)} %copy-done, bf16[16,128,256]{2,1,0:T(8,128)(2,1)S(1)} %bitcast.8, bf16[4,128,384]{2,1,0:T(8,128)(2,1)S(1)} %bitcast.9), custom_call_target="tpu_custom_call" | custom-call | tf_op jit(solution)/shard_map/pallas_call | solution.py:392
  37.7 0.7 %copy.13 = bf16[128,512]{1,0:T(8,128)(2,1)} copy(bf16[128,512]{1,0:T(8,128)(2,1)S(1)} %shard_map.55) | data formatting | bytes 262144
Async XLA Ops:
  1.0 1.6 %copy-start = (s32[8,8]{1,0:T(8,128)S(1)}, s32[8,8]{1,0:T(8,128)}, u32[]{:S(2)}) copy-start(s32[8,8]{1,0:T(8,128)} %lists_ref.1) | copy-start | bytes 772
  2.6 0.7 %copy-start.1 = (s32[4]{0:T(128)S(1)}, s32[4]{0:T(128)}, u32[]{:S(2)}) copy-start(s32[4]{0:T(128)} %rank_ref.1) | copy-start | bytes 52
  2.6 0.7 %copy-start.2 = (s32[8]{0:T(128)S(1)}, s32[8]{0:T(128)}, u32[]{:S(2)}) copy-start(s32[8]{0:T(128)} %depth_ref.1) | copy-start | bytes 100

commit v5 on v4

v5 whole, which is shorter than its diff:
```python
import functools
import math

import jax
import jax.numpy as jnp
from jax import lax
from jax.experimental import pallas as pl
from jax.experimental.pallas import tpu as pltpu
from jax.sharding import PartitionSpec as P

HIDDEN = -1e30
FLOOR = -1e29
MESH = pl.DeviceIdType.MESH
LOG2E = math.log2(math.e)


def attend(
    frames,
    members,
    heads,
    rank_ref,
    depth_ref,
    lists_ref,
    past_ref,
    qkv_ref,
    out_ref,
    kv,
    queries,
    bias,
    lse_cols,
    share_out,
    share_in,
    lse_out,
    lse_in,
    local_sem,
    past_send,
    past_recv,
    fwd_send,
    fwd_recv,
    query_send,
    query_recv,
    share_send,
    share_recv,
    lse_send,
    lse_recv,
):
    toks = past_ref.shape[1]
    dim = past_ref.shape[2] // 2
    scale = LOG2E / math.sqrt(dim)
    fi = lax.axis_index("frame")
    si = lax.axis_index("space")
    group = si // 2
    core = si % 2
    beside = group * 2 + 1 - core
    peer = (fi, beside)
    size = members // 2
    half = group // size
    place = group - half * size
    passes = jnp.logical_or(group == 1, group == members - 2)
    end_from = jnp.where(group == 1, members - 1, 0)
    end_to = members - 1 - end_from

    def frame_at(slot):
        return lax.rem(fi + slot, frames)

    def device_of(member):
        return (fi, member * 2 + core)

    def remote(src, dst, send_sem, recv_sem, device):
        return pltpu.make_async_remote_copy(
            src_ref=src,
            dst_ref=dst,
            send_sem=send_sem,
            recv_sem=recv_sem,
            device_id=device,
            device_id_type=MESH,
        )

    def own_past(h):
        return past_ref.at[fi * heads + h]

    def own_now(h):
        return qkv_ref.at[h, :, pl.ds(dim, 2 * dim)]

    def own_query(h):
        return qkv_ref.at[h, :, pl.ds(0, dim)]

    def local_copies(h):
        return [
            pltpu.make_async_copy(own_past(h), kv.at[0, h, 0], local_sem.at[h, 0]),
            pltpu.make_async_copy(own_now(h), kv.at[0, h, frames], local_sem.at[h, 1]),
            pltpu.make_async_copy(own_query(h), queries.at[h, group], local_sem.at[h, 2]),
        ]

    def each(count, step):
        lax.fori_loop(0, count, lambda at, carry: (step(at), carry)[1], 0)

    def past_copy(h, j):
        to = frame_at(frames - j)
        return remote(
            past_ref.at[to * heads + h],
            kv.at[0, h, j],
            past_send.at[h, j],
            past_recv.at[h, j],
            (to, si),
        )

    def forward(h, j):
        src = kv.at[0, h, j]
        if j == 0:
            src = own_past(h)
        elif j == frames:
            src = own_now(h)
        return remote(src, kv.at[1, h, j], fwd_send.at[h, j], fwd_recv.at[h, j], peer)

    def query_copy(h, j):
        to = lax.rem(group + j, members)
        return jnp.abs(to - group) != members - 1, remote(
            own_query(h),
            queries.at[h, group],
            query_send.at[h, j],
            query_recv.at[h, group],
            device_of(to),
        )

    def query_on(h):
        return remote(
            queries.at[h, end_from],
            queries.at[h, end_from],
            query_send.at[h, 0],
            query_recv.at[h, end_from],
            device_of(end_to),
        )

    def query_wait(h, member):
        remote(
            queries.at[h, member],
            queries.at[h, member],
            query_send.at[h, 0],
            query_recv.at[h, member],
            peer,
        ).wait_recv()

    def start_past(h):
        for j in range(1, frames):
            past_copy(h, j).start()

    def start_query(h):
        for j in range(1, members):
            wanted, copy = query_copy(h, j)
            pl.when(wanted)(copy.start)

    barrier = pltpu.get_barrier_semaphore()
    partners = [(frame_at(j), si) for j in range(1, frames)]
    partners += [device_of(lax.rem(group + j, members)) for j in range(1, members)]
    partners.append(peer)
    for partner in partners:
        pl.semaphore_signal(barrier, inc=1, device_id=partner, device_id_type=MESH)
    pl.semaphore_wait(barrier, len(partners))

    def start_head(h):
        start_past(h)
        start_query(h)
        for j in (0, frames):
            forward(h, j).start()
        for copy in local_copies(h):
            copy.start()

    each(heads, start_head)
    lse_cols[...] = jnp.zeros_like(lse_cols)
    lanes = lax.broadcasted_iota(jnp.int32, (1, toks), 1)

    def bias_of(key_tile, slot, tile):
        sees = lists_ref[tile, key_tile] > 0
        if slot < frames:
            sees = jnp.logical_and(
                sees, rank_ref[frame_at(slot)] >= frames - depth_ref[tile]
            )
        return jnp.where(sees, 0.0, HIDDEN)

    blocks = [(side, slot) for side in range(2) for slot in range(frames + 1)]

    def set_bias(member):
        for at, (side, slot) in enumerate(blocks):
            bias[member, at] = bias_of((si, beside)[side], slot, member * 2 + core)

    each(members, set_bias)

    def share_copy(h, member):
        return remote(
            share_out.at[h, member],
            share_in.at[h, group],
            share_send.at[h, member],
            share_recv.at[h, group],
            device_of(member),
        )

    def unit(h, pair):
        query = queries[h, pl.ds(2 * pair, 2)].reshape(2 * toks, dim)
        keys = kv[:, h, :, :, :dim].reshape(len(blocks) * toks, dim)
        values = kv[:, h, :, :, dim:].reshape(len(blocks) * toks, dim)
        score = lax.dot_general(
            query, keys, (((1,), (1,)), ((), ())), preferred_element_type=jnp.float32
        )
        weights = []
        safes = []
        for at in range(2):
            member = 2 * pair + at
            rows = score[at * toks : (at + 1) * toks]
            parts = [
                rows[:, b * toks : (b + 1) * toks] + bias[member, b] for b in range(len(blocks))
            ]
            peak = jnp.max(functools.reduce(jnp.maximum, parts), axis=1, keepdims=True)
            peak = jnp.maximum(peak, FLOOR) * scale
            parts = [jnp.exp2(part * scale - peak) for part in parts]
            total = jnp.sum(functools.reduce(jnp.add, parts), axis=1, keepdims=True)
            safe = jnp.maximum(total, 1.0)
            safes.append(safe)
            lse = peak + jnp.log(safe) * LOG2E
            lse_cols[member] = jnp.where(lanes == h, lse, lse_cols[member])
            weights.append(jnp.concatenate([part.astype(jnp.bfloat16) for part in parts], 1))
        weighted = jnp.dot(
            jnp.concatenate(weights, 0), values, preferred_element_type=jnp.float32
        )
        for at in range(2):
            member = 2 * pair + at
            share = weighted[at * toks : (at + 1) * toks] * (1.0 / safes[at])
            share_out[h, member] = share.astype(jnp.bfloat16)
            pl.when(member != group)(share_copy(h, member).start)

    def pass_on(h):
        for j in range(1, frames):
            past_copy(h, j).wait_recv()
            forward(h, j).start()

    def head(h):
        for copy in local_copies(h):
            copy.wait()
        for j in range(frames + 1):
            forward(h, j).wait_recv()

        def step(k):
            pair = lax.rem((1 - half) * (size // 2) + k, size)
            for at in range(2):
                member = 2 * pair + at
                pl.when(member != group)(functools.partial(query_wait, h, member))

                @pl.when(jnp.logical_and(passes, member == end_from))
                def _():
                    query_on(h).start()

            unit(h, pair)

            @pl.when(jnp.logical_and(k == 0, h + 1 < heads))
            def _():
                pass_on(h + 1)

        each(size, step)

    pass_on(0)
    each(heads, head)

    for member in range(members):
        lse_out[member] = lse_cols[member].T[: lse_out.shape[1]]

    def lse_copy(j):
        member = lax.rem(group + j, members)
        return remote(
            lse_out.at[member],
            lse_in.at[group],
            lse_send.at[member],
            lse_recv.at[group],
            device_of(member),
        )

    for j in range(1, members):
        lse_copy(j).start()

    def arrived(j):
        member = lax.rem(group + j, members)
        return member, remote(
            lse_out.at[member], lse_in.at[member], lse_send.at[member], lse_recv.at[member], peer
        )

    for j in range(1, members):
        arrived(j)[1].wait_recv()
    rows = [lse_out[group]]
    for j in range(1, members):
        rows.append(lse_in[lax.rem(group + j, members)])
    top = functools.reduce(jnp.maximum, rows)
    factors = [jnp.exp2(row - top) for row in rows]
    inverse = 1.0 / functools.reduce(jnp.add, factors)
    columns = [(factor * inverse).T for factor in factors]
    for h in range(heads):
        summed = share_out[h, group].astype(jnp.float32) * columns[0][:, h : h + 1]
        for j in range(1, members):
            member = lax.rem(group + j, members)
            remote(
                share_out.at[h, member],
                share_in.at[h, member],
                share_send.at[h, member],
                share_recv.at[h, member],
                peer,
            ).wait_recv()
            summed += share_in[h, member].astype(jnp.float32) * columns[j][:, h : h + 1]
        out_ref[:, h * dim : (h + 1) * dim] = summed.astype(out_ref.dtype)

    def sent(h):
        for j in range(1, frames):
            past_copy(h, j).wait_send()
        for j in range(frames + 1):
            forward(h, j).wait_send()
        for j in range(1, members):
            wanted, copy = query_copy(h, j)
            pl.when(wanted)(copy.wait_send)
            share_copy(h, lax.rem(group + j, members)).wait_send()
        pl.when(passes)(query_on(h).wait_send)

    each(heads, sent)
    for j in range(1, members):
        lse_copy(j).wait_send()


def body(qkv_now, past_cache, frame_rank, frame_depth, tile_lists):
    toks, heads, width = qkv_now.shape
    dim = width // 3
    frames = lax.axis_size("frame")
    members = lax.axis_size("space") // 2
    past = jnp.transpose(past_cache[0], (1, 0, 2))
    qkv = jnp.transpose(qkv_now, (1, 0, 2))
    lse_rows = -(-heads // 8) * 8
    dma = pltpu.SemaphoreType.DMA
    smem = pl.BlockSpec(memory_space=pltpu.SMEM)
    return pl.pallas_call(
        functools.partial(attend, frames, members, heads),
        out_shape=jax.ShapeDtypeStruct((toks, heads * dim), jnp.bfloat16),
        in_specs=[smem, smem, smem] + [pl.BlockSpec(memory_space=pl.ANY)] * 2,
        out_specs=pl.BlockSpec(memory_space=pltpu.VMEM),
        scratch_shapes=[
            pltpu.VMEM((2, heads, frames + 1, toks, 2 * dim), jnp.bfloat16),
            pltpu.VMEM((heads, members, toks, dim), jnp.bfloat16),
            pltpu.SMEM((members, 2 * (frames + 1)), jnp.float32),
            pltpu.VMEM((members, toks, toks), jnp.float32),
            pltpu.VMEM((heads, members, toks, dim), jnp.bfloat16),
            pltpu.VMEM((heads, members, toks, dim), jnp.bfloat16),
            pltpu.VMEM((members, lse_rows, toks), jnp.float32),
            pltpu.VMEM((members, lse_rows, toks), jnp.float32),
            dma((heads, 3)),
            dma((heads, frames)),
            dma((heads, frames)),
            dma((heads, frames + 1)),
            dma((heads, frames + 1)),
            dma((heads, members)),
            dma((heads, members)),
            dma((heads, members)),
            dma((heads, members)),
            dma((members,)),
            dma((members,)),
        ],
        compiler_params=pltpu.CompilerParams(
            collective_id=0, has_side_effects=True, vmem_limit_bytes=48 * 1024 * 1024
        ),
    )(frame_rank, frame_depth, tile_lists, past, qkv)


def solution(mesh):
    in_specs = (P("space", "frame", None), P("frame", "space", None, None), P(), P(), P())
    out_specs = P("space", "frame")
    return jax.shard_map(body, mesh=mesh, in_specs=in_specs, out_specs=out_specs, check_vma=False)
```

time: 38.5 us -> 39 us (1.013)
  Pallas kernels: 34.4 us -> 34.8 us
    pallas_call x1, Pallas kernels: 34.4 us -> 34.8 us  [body(): pl.pallas_call(functools.partial(attend, frames, members, heads), out_sha...]
where the time goes in v5:
time: 39 us; the launch traced here: 38.8 us
  Pallas kernels  34.8 us (89%)
  local copies, waits for them, and re-layouts  3.92 us (10%)
    pallas_call x1, Pallas kernels, body(): pl.pallas_call(functools.partial(attend, frames, members, heads), out_sha...  34.8 us
    unnamed x9, local copies, waits for them, and re-layouts  3.92 us

profile of v5, /device:TPU:0, one launch (start us, length us, event | category | flops | bytes accessed | tf_op | source)
XLA Modules:
  0.0 38.8 jit_solution(10614044368601722642)
XLA Ops:
  0.0 1.0 %copy.11 = bf16[128,4,384]{2,0,1:T(8,128)(2,1)S(1)} copy(bf16[128,4,384]{2,1,0:T(4,128)(2,1)} %param.5) | data formatting | bytes 786432 | tf_op args[0]
  1.0 0.0 copy-start
  1.1 1.6 %copy.10 = bf16[1,128,16,256]{3,1,2,0:T(8,128)(2,1)S(1)} copy(bf16[1,128,16,256]{3,2,1,0:T(8,128)(2,1)} %param.6) | data formatting | bytes 2097152 | tf_op args[1]
  2.6 0.0 copy-start.1
  2.6 0.0 copy-start.2
  2.7 0.0 copy-done
  2.7 0.6 %copy-done.1 = s32[4]{0:T(128)S(1)} copy-done((s32[4]{0:T(128)S(1)}, s32[4]{0:T(128)}, u32[]{:S(2)}) %copy-start.1) | copy-done | bytes 40
  3.3 0.0 copy-done.2
  3.3 34.8 %shard_map.55 = bf16[128,512]{1,0:T(8,128)(2,1)S(1)} custom-call(s32[4]{0:T(128)S(1)} %copy-done.1, s32[8]{0:T(128)S(1)} %copy-done.2, s32[8,8]{1,0:T(8,128)S(1)} %copy-done, bf16[16,128,256]{2,1,0:T(8,128)(2,1)S(1)} %bitcast.8, bf16[4,128,384]{2,1,0:T(8,128)(2,1)S(1)} %bitcast.9), custom_call_target="tpu_custom_call" | custom-call | tf_op jit(solution)/shard_map/pallas_call | solution.py:334
  38.2 0.7 %copy.13 = bf16[128,512]{1,0:T(8,128)(2,1)} copy(bf16[128,512]{1,0:T(8,128)(2,1)S(1)} %shard_map.55) | data formatting | bytes 262144
Async XLA Ops:
  1.0 1.6 %copy-start = (s32[8,8]{1,0:T(8,128)S(1)}, s32[8,8]{1,0:T(8,128)}, u32[]{:S(2)}) copy-start(s32[8,8]{1,0:T(8,128)} %lists_ref.1) | copy-start | bytes 772
  2.6 0.7 %copy-start.1 = (s32[4]{0:T(128)S(1)}, s32[4]{0:T(128)}, u32[]{:S(2)}) copy-start(s32[4]{0:T(128)} %rank_ref.1) | copy-start | bytes 52
  2.6 0.7 %copy-start.2 = (s32[8]{0:T(128)S(1)}, s32[8]{0:T(128)}, u32[]{:S(2)}) copy-start(s32[8]{0:T(128)} %depth_ref.1) | copy-start | bytes 100

commit v6 on v5

--- a/solution.py
+++ b/solution.py
@@ -14,7 +14,7 @@
 LOG2E = math.log2(math.e)
 
 
-def attend(
+def attend_by_tile(
     frames,
     members,
     heads,
@@ -321,18 +321,16 @@
         lse_copy(j).wait_send()
 
 
-def body(qkv_now, past_cache, frame_rank, frame_depth, tile_lists):
-    toks, heads, width = qkv_now.shape
+def call_by_tile(qkv, past, frame_rank, frame_depth, tile_lists):
+    heads, toks, width = qkv.shape
     dim = width // 3
     frames = lax.axis_size("frame")
     members = lax.axis_size("space") // 2
-    past = jnp.transpose(past_cache[0], (1, 0, 2))
-    qkv = jnp.transpose(qkv_now, (1, 0, 2))
     lse_rows = -(-heads // 8) * 8
     dma = pltpu.SemaphoreType.DMA
     smem = pl.BlockSpec(memory_space=pltpu.SMEM)
     return pl.pallas_call(
-        functools.partial(attend, frames, members, heads),
+        functools.partial(attend_by_tile, frames, members, heads),
         out_shape=jax.ShapeDtypeStruct((toks, heads * dim), jnp.bfloat16),
         in_specs=[smem, smem, smem] + [pl.BlockSpec(memory_space=pl.ANY)] * 2,
         out_specs=pl.BlockSpec(memory_space=pltpu.VMEM),
@@ -363,6 +361,312 @@
     )(frame_rank, frame_depth, tile_lists, past, qkv)
 
 
+def attend_by_head(
+    frames,
+    members,
+    heads,
+    rank_ref,
+    depth_ref,
+    lists_ref,
+    past_ref,
+    qkv_ref,
+    out_ref,
+    kv,
+    queries,
+    bias,
+    lse_cols,
+    share_out,
+    share_in,
+    lse_out,
+    lse_in,
+    local_sem,
+    past_send,
+    past_recv,
+    query_send,
+    query_recv,
+    share_send,
+    share_recv,
+    lse_send,
+    lse_recv,
+):
+    toks = past_ref.shape[1]
+    dim = past_ref.shape[2] // 2
+    own = heads // 2
+    tiles = 2 * members
+    scale = LOG2E / math.sqrt(dim)
+    fi = lax.axis_index("frame")
+    si = lax.axis_index("space")
+    group = si // 2
+    core = si % 2
+    peer = (fi, group * 2 + 1 - core)
+    half = group // (members // 2)
+
+    def frame_at(slot):
+        return lax.rem(fi + slot, frames)
+
+    def core_at(e):
+        return core if e == 0 else 1 - core
+
+    def tile_at(j):
+        return lax.rem(si + j, tiles)
+
+    def remote(src, dst, send_sem, recv_sem, device):
+        return pltpu.make_async_remote_copy(
+            src_ref=src,
+            dst_ref=dst,
+            send_sem=send_sem,
+            recv_sem=recv_sem,
+            device_id=device,
+            device_id_type=MESH,
+        )
+
+    def each(count, step):
+        lax.fori_loop(0, count, lambda at, carry: (step(at), carry)[1], 0)
+
+    def past_source(h, e, j):
+        to = fi if j in (0, frames) else frame_at(frames - j)
+        head = core_at(e) * own + h
+        if j == frames:
+            return to, qkv_ref.at[head, :, pl.ds(dim, 2 * dim)]
+        return to, past_ref.at[to * heads + head]
+
+    def query_source(h, to_core):
+        return qkv_ref.at[to_core * own + h, :, pl.ds(0, dim)]
+
+    def local_copies(h):
+        return [
+            pltpu.make_async_copy(past_source(h, 0, 0)[1], kv.at[h, core, 0], local_sem.at[h, 0]),
+            pltpu.make_async_copy(
+                past_source(h, 0, frames)[1], kv.at[h, core, frames], local_sem.at[h, 1]
+            ),
+            pltpu.make_async_copy(query_source(h, core), queries.at[h, si], local_sem.at[h, 2]),
+        ]
+
+    sent_blocks = [(e, j) for j in range(1, frames) for e in range(2)] + [(1, 0), (1, frames)]
+
+    def past_copy(h, e, j):
+        to, src = past_source(h, e, j)
+        return remote(
+            src,
+            kv.at[h, core, j],
+            past_send.at[h, e, j],
+            past_recv.at[h, core, j],
+            (to, group * 2 + core_at(e)),
+        )
+
+    def past_wait(h, e, j):
+        block = kv.at[h, core_at(e), j]
+        remote(block, block, past_send.at[h, e, j], past_recv.at[h, core_at(e), j], peer).wait_recv()
+
+    def query_copy(h, j):
+        to = tile_at(j)
+        return remote(
+            query_source(h, lax.rem(to, 2)),
+            queries.at[h, si],
+            query_send.at[h, j],
+            query_recv.at[h, si],
+            (fi, to),
+        )
+
+    def query_wait(h, tile):
+        block = queries.at[h, tile]
+        remote(block, block, query_send.at[h, 0], query_recv.at[h, tile], peer).wait_recv()
+
+    barrier = pltpu.get_barrier_semaphore()
+    partners = [(frame_at(j), group * 2 + e) for j in range(1, frames) for e in range(2)]
+    partners += [(fi, tile_at(j)) for j in range(1, tiles)]
+    for partner in partners:
+        pl.semaphore_signal(barrier, inc=1, device_id=partner, device_id_type=MESH)
+    pl.semaphore_wait(barrier, len(partners))
+
+    def start_head(h):
+        for e, j in sent_blocks:
+            past_copy(h, e, j).start()
+        for j in range(1, tiles):
+            query_copy(h, j).start()
+        for copy in local_copies(h):
+            copy.start()
+
+    each(own, start_head)
+
+    lse_cols[...] = jnp.zeros_like(lse_cols)
+    lanes = lax.broadcasted_iota(jnp.int32, (1, toks), 1)
+
+    def bias_of(key_tile, slot, tile):
+        sees = lists_ref[tile, key_tile] > 0
+        if slot < frames:
+            sees = jnp.logical_and(
+                sees, rank_ref[frame_at(slot)] >= frames - depth_ref[tile]
+            )
+        return jnp.where(sees, 0.0, HIDDEN)
+
+    blocks = [(side, slot) for side in range(2) for slot in range(frames + 1)]
+
+    def set_bias(tile):
+        for at, (side, slot) in enumerate(blocks):
+            bias[tile, at] = bias_of(group * 2 + side, slot, tile)
+
+    each(tiles, set_bias)
+
+    def share_copy(h, tile):
+        return remote(
+            share_out.at[h, tile],
+            share_in.at[core * own + h, group],
+            share_send.at[h, tile],
+            share_recv.at[core * own + h, group],
+            (fi, tile),
+        )
+
+    def unit(h, member):
+        query = queries[h, pl.ds(2 * member, 2)].reshape(2 * toks, dim)
+        keys = kv[h, :, :, :, :dim].reshape(len(blocks) * toks, dim)
+        values = kv[h, :, :, :, dim:].reshape(len(blocks) * toks, dim)
+        score = lax.dot_general(
+            query, keys, (((1,), (1,)), ((), ())), preferred_element_type=jnp.float32
+        )
+        weights = []
+        safes = []
+        for at in range(2):
+            tile = 2 * member + at
+            rows = score[at * toks : (at + 1) * toks]
+            parts = [
+                rows[:, b * toks : (b + 1) * toks] + bias[tile, b] for b in range(len(blocks))
+            ]
+            peak = jnp.max(functools.reduce(jnp.maximum, parts), axis=1, keepdims=True)
+            peak = jnp.maximum(peak, FLOOR) * scale
+            parts = [jnp.exp2(part * scale - peak) for part in parts]
+            total = jnp.sum(functools.reduce(jnp.add, parts), axis=1, keepdims=True)
+            safe = jnp.maximum(total, 1.0)
+            safes.append(safe)
+            lse = peak + jnp.log(safe) * LOG2E
+            lse_cols[tile] = jnp.where(lanes == h, lse, lse_cols[tile])
+            weights.append(jnp.concatenate([part.astype(jnp.bfloat16) for part in parts], 1))
+        weighted = jnp.dot(
+            jnp.concatenate(weights, 0), values, preferred_element_type=jnp.float32
+        )
+        for at in range(2):
+            tile = 2 * member + at
+            share = weighted[at * toks : (at + 1) * toks] * (1.0 / safes[at])
+            share_out[h, tile] = share.astype(jnp.bfloat16)
+            pl.when(tile != si)(share_copy(h, tile).start)
+
+    def head(h):
+        for copy in local_copies(h):
+            copy.wait()
+        for e, j in sent_blocks:
+            past_wait(h, e, j)
+
+        def step(k):
+            member = lax.rem((1 - half) * (members // 2) + k, members)
+            for at in range(2):
+                tile = 2 * member + at
+                pl.when(tile != si)(functools.partial(query_wait, h, tile))
+            unit(h, member)
+
+        each(members, step)
+
+    each(own, head)
+
+    for tile in range(tiles):
+        lse_out[tile] = lse_cols[tile].T[: lse_out.shape[1]]
+
+    def lse_copy(j):
+        tile = tile_at(j)
+        return remote(
+            lse_out.at[tile],
+            lse_in.at[core, group],
+            lse_send.at[tile],
+            lse_recv.at[core, group],
+            (fi, tile),
+        )
+
+    for j in range(1, tiles):
+        lse_copy(j).start()
+    lse_in[core, group] = lse_out[si]
+    for h in range(own):
+        share_in[core * own + h, group] = share_out[h, si]
+    for j in range(1, tiles):
+        tile = tile_at(j)
+        block = lse_in.at[lax.rem(tile, 2), tile // 2]
+        remote(
+            block, block, lse_send.at[tile], lse_recv.at[lax.rem(tile, 2), tile // 2], peer
+        ).wait_recv()
+    for c in range(2):
+        rows = [lse_in[c, m] for m in range(members)]
+        top = functools.reduce(jnp.maximum, rows)
+        factors = [jnp.exp2(row - top) for row in rows]
+        inverse = 1.0 / functools.reduce(jnp.add, factors)
+        columns = [(factor * inverse).T for factor in factors]
+        for h in range(own):
+            at = c * own + h
+            summed = 0.0
+            for m in range(members):
+                block = share_in.at[at, m]
+                pl.when(2 * m + c != si)(
+                    remote(block, block, share_send.at[h, 0], share_recv.at[at, m], peer).wait_recv
+                )
+                summed += share_in[at, m].astype(jnp.float32) * columns[m][:, h : h + 1]
+            out_ref[:, at * dim : (at + 1) * dim] = summed.astype(out_ref.dtype)
+
+    def sent(h):
+        for e, j in sent_blocks:
+            past_copy(h, e, j).wait_send()
+        for j in range(1, tiles):
+            query_copy(h, j).wait_send()
+            share_copy(h, tile_at(j)).wait_send()
+
+    each(own, sent)
+    for j in range(1, tiles):
+        lse_copy(j).wait_send()
+
+
+def call_by_head(qkv, past, frame_rank, frame_depth, tile_lists):
+    heads, toks, width = qkv.shape
+    dim = width // 3
+    frames = lax.axis_size("frame")
+    tiles = lax.axis_size("space")
+    members = tiles // 2
+    own = heads // 2
+    lse_rows = -(-own // 8) * 8
+    dma = pltpu.SemaphoreType.DMA
+    smem = pl.BlockSpec(memory_space=pltpu.SMEM)
+    return pl.pallas_call(
+        functools.partial(attend_by_head, frames, members, heads),
+        out_shape=jax.ShapeDtypeStruct((toks, heads * dim), jnp.bfloat16),
+        in_specs=[smem, smem, smem] + [pl.BlockSpec(memory_space=pl.ANY)] * 2,
+        out_specs=pl.BlockSpec(memory_space=pltpu.VMEM),
+        scratch_shapes=[
+            pltpu.VMEM((own, 2, frames + 1, toks, 2 * dim), jnp.bfloat16),
+            pltpu.VMEM((own, tiles, toks, dim), jnp.bfloat16),
+            pltpu.SMEM((tiles, 2 * (frames + 1)), jnp.float32),
+            pltpu.VMEM((tiles, toks, toks), jnp.float32),
+            pltpu.VMEM((own, tiles, toks, dim), jnp.bfloat16),
+            pltpu.VMEM((heads, members, toks, dim), jnp.bfloat16),
+            pltpu.VMEM((tiles, lse_rows, toks), jnp.float32),
+            pltpu.VMEM((2, members, lse_rows, toks), jnp.float32),
+            dma((own, 3)),
+            dma((own, 2, frames + 1)),
+            dma((own, 2, frames + 1)),
+            dma((own, tiles)),
+            dma((own, tiles)),
+            dma((own, tiles)),
+            dma((heads, members)),
+            dma((tiles,)),
+            dma((2, members)),
+        ],
+        compiler_params=pltpu.CompilerParams(
+            collective_id=0, has_side_effects=True, vmem_limit_bytes=48 * 1024 * 1024
+        ),
+    )(frame_rank, frame_depth, tile_lists, past, qkv)
+
+
+def body(qkv_now, past_cache, frame_rank, frame_depth, tile_lists):
+    past = jnp.transpose(past_cache[0], (1, 0, 2))
+    qkv = jnp.transpose(qkv_now, (1, 0, 2))
+    call = call_by_tile if qkv.shape[0] % 2 else call_by_head
+    return call(qkv, past, frame_rank, frame_depth, tile_lists)
+
+
 def solution(mesh):
     in_specs = (P("space", "frame", None), P("frame", "space", None, None), P(), P(), P())
     out_specs = P("space", "frame")

time: 39 us -> 38.2 us (0.979)
  Pallas kernels: 34.8 us -> 34 us
    pallas_call x1, Pallas kernels: 34.8 us -> 34 us  [call_by_head(): pl.pallas_call(functools.partial(attend_by_head, frames, members, heads),...]
where the time goes in v6:
time: 38.2 us; the launch traced here: 38 us
  Pallas kernels  34 us (89%)
  local copies, waits for them, and re-layouts  3.92 us (10%)
    pallas_call x1, Pallas kernels, call_by_head(): pl.pallas_call(functools.partial(attend_by_head, frames, members, heads),...  34 us
    unnamed x9, local copies, waits for them, and re-layouts  3.92 us

profile of v6, /device:TPU:0, one launch (start us, length us, event | category | flops | bytes accessed | tf_op | source)
XLA Modules:
  0.0 38.0 jit_solution(5522269362099450616)
XLA Ops:
  0.0 1.0 %copy.11 = bf16[128,4,384]{2,0,1:T(8,128)(2,1)S(1)} copy(bf16[128,4,384]{2,1,0:T(4,128)(2,1)} %param.5) | data formatting | bytes 786432 | tf_op args[0]
  1.0 0.0 copy-start
  1.1 1.6 %copy.10 = bf16[1,128,16,256]{3,1,2,0:T(8,128)(2,1)S(1)} copy(bf16[1,128,16,256]{3,2,1,0:T(8,128)(2,1)} %param.6) | data formatting | bytes 2097152 | tf_op args[1]
  2.6 0.0 copy-start.1
  2.6 0.0 copy-start.2
  2.7 0.0 copy-done
  2.7 0.6 %copy-done.1 = s32[4]{0:T(128)S(1)} copy-done((s32[4]{0:T(128)S(1)}, s32[4]{0:T(128)}, u32[]{:S(2)}) %copy-start.1) | copy-done | bytes 40
  3.3 0.0 copy-done.2
  3.3 34.0 %shard_map.55 = bf16[128,512]{1,0:T(8,128)(2,1)S(1)} custom-call(s32[4]{0:T(128)S(1)} %copy-done.1, s32[8]{0:T(128)S(1)} %copy-done.2, s32[8,8]{1,0:T(8,128)S(1)} %copy-done, bf16[16,128,256]{2,1,0:T(8,128)(2,1)S(1)} %bitcast.8, bf16[4,128,384]{2,1,0:T(8,128)(2,1)S(1)} %bitcast.9), custom_call_target="tpu_custom_call" | custom-call | tf_op jit(solution)/shard_map/pallas_call | solution.py:633
  37.3 0.7 %copy.13 = bf16[128,512]{1,0:T(8,128)(2,1)} copy(bf16[128,512]{1,0:T(8,128)(2,1)S(1)} %shard_map.55) | data formatting | bytes 262144
Async XLA Ops:
  1.0 1.6 %copy-start = (s32[8,8]{1,0:T(8,128)S(1)}, s32[8,8]{1,0:T(8,128)}, u32[]{:S(2)}) copy-start(s32[8,8]{1,0:T(8,128)} %lists_ref.1) | copy-start | bytes 772
  2.6 0.7 %copy-start.1 = (s32[4]{0:T(128)S(1)}, s32[4]{0:T(128)}, u32[]{:S(2)}) copy-start(s32[4]{0:T(128)} %rank_ref.1) | copy-start | bytes 52
  2.6 0.7 %copy-start.2 = (s32[8]{0:T(128)S(1)}, s32[8]{0:T(128)}, u32[]{:S(2)}) copy-start(s32[8]{0:T(128)} %depth_ref.1) | copy-start | bytes 100

commit v7 on v6

--- a/solution.py
+++ b/solution.py
@@ -423,54 +423,50 @@
     def each(count, step):
         lax.fori_loop(0, count, lambda at, carry: (step(at), carry)[1], 0)
 
-    def past_source(h, e, j):
+    def past_source(e, j):
         to = fi if j in (0, frames) else frame_at(frames - j)
-        head = core_at(e) * own + h
         if j == frames:
-            return to, qkv_ref.at[head, :, pl.ds(dim, 2 * dim)]
-        return to, past_ref.at[to * heads + head]
-
-    def query_source(h, to_core):
-        return qkv_ref.at[to_core * own + h, :, pl.ds(0, dim)]
-
-    def local_copies(h):
-        return [
-            pltpu.make_async_copy(past_source(h, 0, 0)[1], kv.at[h, core, 0], local_sem.at[h, 0]),
-            pltpu.make_async_copy(
-                past_source(h, 0, frames)[1], kv.at[h, core, frames], local_sem.at[h, 1]
-            ),
-            pltpu.make_async_copy(query_source(h, core), queries.at[h, si], local_sem.at[h, 2]),
-        ]
+            return to, qkv_ref.at[pl.ds(core_at(e) * own, own), :, pl.ds(dim, 2 * dim)]
+        return to, past_ref.at[pl.ds(to * heads + core_at(e) * own, own)]
+
+    def query_source(to_core):
+        return qkv_ref.at[pl.ds(to_core * own, own), :, pl.ds(0, dim)]
+
+    local = [
+        pltpu.make_async_copy(past_source(0, 0)[1], kv.at[core, 0], local_sem.at[0]),
+        pltpu.make_async_copy(past_source(0, frames)[1], kv.at[core, frames], local_sem.at[1]),
+        pltpu.make_async_copy(query_source(core), queries.at[si], local_sem.at[2]),
+    ]
 
     sent_blocks = [(e, j) for j in range(1, frames) for e in range(2)] + [(1, 0), (1, frames)]
 
-    def past_copy(h, e, j):
-        to, src = past_source(h, e, j)
+    def past_copy(e, j):
+        to, src = past_source(e, j)
         return remote(
             src,
-            kv.at[h, core, j],
-            past_send.at[h, e, j],
-            past_recv.at[h, core, j],
+            kv.at[core, j],
+            past_send.at[e, j],
+            past_recv.at[core, j],
             (to, group * 2 + core_at(e)),
         )
 
-    def past_wait(h, e, j):
-        block = kv.at[h, core_at(e), j]
-        remote(block, block, past_send.at[h, e, j], past_recv.at[h, core_at(e), j], peer).wait_recv()
-
-    def query_copy(h, j):
+    def past_wait(e, j):
+        block = kv.at[core_at(e), j]
+        remote(block, block, past_send.at[e, j], past_recv.at[core_at(e), j], peer).wait_recv()
+
+    def query_copy(j):
         to = tile_at(j)
         return remote(
-            query_source(h, lax.rem(to, 2)),
-            queries.at[h, si],
-            query_send.at[h, j],
-            query_recv.at[h, si],
+            query_source(lax.rem(to, 2)),
+            queries.at[si],
+            query_send.at[j],
+            query_recv.at[si],
             (fi, to),
         )
 
-    def query_wait(h, tile):
-        block = queries.at[h, tile]
-        remote(block, block, query_send.at[h, 0], query_recv.at[h, tile], peer).wait_recv()
+    def query_wait(tile):
+        block = queries.at[tile]
+        remote(block, block, query_send.at[0], query_recv.at[tile], peer).wait_recv()
 
     barrier = pltpu.get_barrier_semaphore()
     partners = [(frame_at(j), group * 2 + e) for j in range(1, frames) for e in range(2)]
@@ -479,15 +475,12 @@
         pl.semaphore_signal(barrier, inc=1, device_id=partner, device_id_type=MESH)
     pl.semaphore_wait(barrier, len(partners))
 
-    def start_head(h):
-        for e, j in sent_blocks:
-            past_copy(h, e, j).start()
-        for j in range(1, tiles):
-            query_copy(h, j).start()
-        for copy in local_copies(h):
-            copy.start()
-
-    each(own, start_head)
+    for e, j in sent_blocks:
+        past_copy(e, j).start()
+    for j in range(1, tiles):
+        query_copy(j).start()
+    for copy in local:
+        copy.start()
 
     lse_cols[...] = jnp.zeros_like(lse_cols)
     lanes = lax.broadcasted_iota(jnp.int32, (1, toks), 1)
@@ -508,19 +501,19 @@
 
     each(tiles, set_bias)
 
-    def share_copy(h, tile):
-        return remote(
-            share_out.at[h, tile],
-            share_in.at[core * own + h, group],
-            share_send.at[h, tile],
-            share_recv.at[core * own + h, group],
+    def share_copy(tile):
+        return remote(
+            share_out.at[tile],
+            share_in.at[core, group],
+            share_send.at[tile],
+            share_recv.at[core, group],
             (fi, tile),
         )
 
     def unit(h, member):
-        query = queries[h, pl.ds(2 * member, 2)].reshape(2 * toks, dim)
-        keys = kv[h, :, :, :, :dim].reshape(len(blocks) * toks, dim)
-        values = kv[h, :, :, :, dim:].reshape(len(blocks) * toks, dim)
+        query = queries[pl.ds(2 * member, 2), h].reshape(2 * toks, dim)
+        keys = kv[:, :, h, :, :dim].reshape(len(blocks) * toks, dim)
+        values = kv[:, :, h, :, dim:].reshape(len(blocks) * toks, dim)
         score = lax.dot_general(
             query, keys, (((1,), (1,)), ((), ())), preferred_element_type=jnp.float32
         )
@@ -547,25 +540,24 @@
         for at in range(2):
             tile = 2 * member + at
             share = weighted[at * toks : (at + 1) * toks] * (1.0 / safes[at])
-            share_out[h, tile] = share.astype(jnp.bfloat16)
-            pl.when(tile != si)(share_copy(h, tile).start)
-
-    def head(h):
-        for copy in local_copies(h):
-            copy.wait()
-        for e, j in sent_blocks:
-            past_wait(h, e, j)
-
-        def step(k):
-            member = lax.rem((1 - half) * (members // 2) + k, members)
-            for at in range(2):
-                tile = 2 * member + at
-                pl.when(tile != si)(functools.partial(query_wait, h, tile))
-            unit(h, member)
-
-        each(members, step)
-
-    each(own, head)
+            share_out[tile, h] = share.astype(jnp.bfloat16)
+
+    for copy in local:
+        copy.wait()
+    for e, j in sent_blocks:
+        past_wait(e, j)
+
+    def step(k):
+        member = lax.rem((1 - half) * (members // 2) + k, members)
+        for at in range(2):
+            tile = 2 * member + at
+            pl.when(tile != si)(functools.partial(query_wait, tile))
+        each(own, lambda h: unit(h, member))
+        for at in range(2):
+            tile = 2 * member + at
+            pl.when(tile != si)(share_copy(tile).start)
+
+    each(members, step)
 
     for tile in range(tiles):
         lse_out[tile] = lse_cols[tile].T[: lse_out.shape[1]]
@@ -583,8 +575,7 @@
     for j in range(1, tiles):
         lse_copy(j).start()
     lse_in[core, group] = lse_out[si]
-    for h in range(own):
-        share_in[core * own + h, group] = share_out[h, si]
+    share_in[core, group] = share_out[si]
     for j in range(1, tiles):
         tile = tile_at(j)
         block = lse_in.at[lax.rem(tile, 2), tile // 2]
@@ -597,26 +588,23 @@
         factors = [jnp.exp2(row - top) for row in rows]
         inverse = 1.0 / functools.reduce(jnp.add, factors)
         columns = [(factor * inverse).T for factor in factors]
+        for m in range(members):
+            block = share_in.at[c, m]
+            pl.when(2 * m + c != si)(
+                remote(block, block, share_send.at[0], share_recv.at[c, m], peer).wait_recv
+            )
         for h in range(own):
             at = c * own + h
             summed = 0.0
             for m in range(members):
-                block = share_in.at[at, m]
-                pl.when(2 * m + c != si)(
-                    remote(block, block, share_send.at[h, 0], share_recv.at[at, m], peer).wait_recv
-                )
-                summed += share_in[at, m].astype(jnp.float32) * columns[m][:, h : h + 1]
+                summed += share_in[c, m, h].astype(jnp.float32) * columns[m][:, h : h + 1]
             out_ref[:, at * dim : (at + 1) * dim] = summed.astype(out_ref.dtype)
 
-    def sent(h):
-        for e, j in sent_blocks:
-            past_copy(h, e, j).wait_send()
-        for j in range(1, tiles):
-            query_copy(h, j).wait_send()
-            share_copy(h, tile_at(j)).wait_send()
-
-    each(own, sent)
+    for e, j in sent_blocks:
+        past_copy(e, j).wait_send()
     for j in range(1, tiles):
+        query_copy(j).wait_send()
+        share_copy(tile_at(j)).wait_send()
         lse_copy(j).wait_send()
 
 
@@ -636,21 +624,21 @@
         in_specs=[smem, smem, smem] + [pl.BlockSpec(memory_space=pl.ANY)] * 2,
         out_specs=pl.BlockSpec(memory_space=pltpu.VMEM),
         scratch_shapes=[
-            pltpu.VMEM((own, 2, frames + 1, toks, 2 * dim), jnp.bfloat16),
-            pltpu.VMEM((own, tiles, toks, dim), jnp.bfloat16),
+            pltpu.VMEM((2, frames + 1, own, toks, 2 * dim), jnp.bfloat16),
+            pltpu.VMEM((tiles, own, toks, dim), jnp.bfloat16),
             pltpu.SMEM((tiles, 2 * (frames + 1)), jnp.float32),
             pltpu.VMEM((tiles, toks, toks), jnp.float32),
-            pltpu.VMEM((own, tiles, toks, dim), jnp.bfloat16),
-            pltpu.VMEM((heads, members, toks, dim), jnp.bfloat16),
+            pltpu.VMEM((tiles, own, toks, dim), jnp.bfloat16),
+            pltpu.VMEM((2, members, own, toks, dim), jnp.bfloat16),
             pltpu.VMEM((tiles, lse_rows, toks), jnp.float32),
             pltpu.VMEM((2, members, lse_rows, toks), jnp.float32),
-            dma((own, 3)),
-            dma((own, 2, frames + 1)),
-            dma((own, 2, frames + 1)),
-            dma((own, tiles)),
-            dma((own, tiles)),
-            dma((own, tiles)),
-            dma((heads, members)),
+            dma((3,)),
+            dma((2, frames + 1)),
+            dma((2, frames + 1)),
+            dma((tiles,)),
+            dma((tiles,)),
+            dma((tiles,)),
+            dma((2, members)),
             dma((tiles,)),
             dma((2, members)),
         ],

time: 38.2 us -> 40.6 us (1.063)
  Pallas kernels: 34 us -> 36.4 us
    pallas_call x1, Pallas kernels: 34 us -> 36.4 us  [call_by_head(): pl.pallas_call(functools.partial(attend_by_head, frames, members, heads),...]
where the time goes in v7:
time: 40.6 us; the launch traced here: 40.4 us
  Pallas kernels  36.4 us (90%)
  local copies, waits for them, and re-layouts  3.92 us (10%)
    pallas_call x1, Pallas kernels, call_by_head(): pl.pallas_call(functools.partial(attend_by_head, frames, members, heads),...  36.4 us
    unnamed x9, local copies, waits for them, and re-layouts  3.92 us

profile of v7, /device:TPU:0, one launch (start us, length us, event | category | flops | bytes accessed | tf_op | source)
XLA Modules:
  0.0 40.4 jit_solution(11368333295811176806)
XLA Ops:
  0.0 1.0 %copy.11 = bf16[128,4,384]{2,0,1:T(8,128)(2,1)S(1)} copy(bf16[128,4,384]{2,1,0:T(4,128)(2,1)} %param.5) | data formatting | bytes 786432 | tf_op args[0]
  1.0 0.0 copy-start
  1.1 1.6 %copy.10 = bf16[1,128,16,256]{3,1,2,0:T(8,128)(2,1)S(1)} copy(bf16[1,128,16,256]{3,2,1,0:T(8,128)(2,1)} %param.6) | data formatting | bytes 2097152 | tf_op args[1]
  2.6 0.0 copy-start.1
  2.6 0.0 copy-start.2
  2.7 0.0 copy-done
  2.7 0.6 %copy-done.1 = s32[4]{0:T(128)S(1)} copy-done((s32[4]{0:T(128)S(1)}, s32[4]{0:T(128)}, u32[]{:S(2)}) %copy-start.1) | copy-done | bytes 40
  3.3 0.0 copy-done.2
  3.3 36.4 %shard_map.55 = bf16[128,512]{1,0:T(8,128)(2,1)S(1)} custom-call(s32[4]{0:T(128)S(1)} %copy-done.1, s32[8]{0:T(128)S(1)} %copy-done.2, s32[8,8]{1,0:T(8,128)S(1)} %copy-done, bf16[16,128,256]{2,1,0:T(8,128)(2,1)S(1)} %bitcast.8, bf16[4,128,384]{2,1,0:T(8,128)(2,1)S(1)} %bitcast.9), custom_call_target="tpu_custom_call" | custom-call | tf_op jit(solution)/shard_map/pallas_call | solution.py:621
  39.7 0.7 %copy.13 = bf16[128,512]{1,0:T(8,128)(2,1)} copy(bf16[128,512]{1,0:T(8,128)(2,1)S(1)} %shard_map.55) | data formatting | bytes 262144
Async XLA Ops:
  1.0 1.6 %copy-start = (s32[8,8]{1,0:T(8,128)S(1)}, s32[8,8]{1,0:T(8,128)}, u32[]{:S(2)}) copy-start(s32[8,8]{1,0:T(8,128)} %lists_ref.1) | copy-start | bytes 772
  2.6 0.7 %copy-start.1 = (s32[4]{0:T(128)S(1)}, s32[4]{0:T(128)}, u32[]{:S(2)}) copy-start(s32[4]{0:T(128)} %rank_ref.1) | copy-start | bytes 52
  2.6 0.7 %copy-start.2 = (s32[8]{0:T(128)S(1)}, s32[8]{0:T(128)}, u32[]{:S(2)}) copy-start(s32[8]{0:T(128)} %depth_ref.1) | copy-start | bytes 100

commit v8 on v5

--- a/solution.py
+++ b/solution.py
@@ -55,10 +55,6 @@
     peer = (fi, beside)
     size = members // 2
     half = group // size
-    place = group - half * size
-    passes = jnp.logical_or(group == 1, group == members - 2)
-    end_from = jnp.where(group == 1, members - 1, 0)
-    end_to = members - 1 - end_from
 
     def frame_at(slot):
         return lax.rem(fi + slot, frames)
@@ -115,21 +111,12 @@
 
     def query_copy(h, j):
         to = lax.rem(group + j, members)
-        return jnp.abs(to - group) != members - 1, remote(
+        return remote(
             own_query(h),
             queries.at[h, group],
             query_send.at[h, j],
             query_recv.at[h, group],
             device_of(to),
-        )
-
-    def query_on(h):
-        return remote(
-            queries.at[h, end_from],
-            queries.at[h, end_from],
-            query_send.at[h, 0],
-            query_recv.at[h, end_from],
-            device_of(end_to),
         )
 
     def query_wait(h, member):
@@ -147,8 +134,8 @@
 
     def start_query(h):
         for j in range(1, members):
-            wanted, copy = query_copy(h, j)
-            pl.when(wanted)(copy.start)
+            query_copy(h, j).start()
+
 
     barrier = pltpu.get_barrier_semaphore()
     partners = [(frame_at(j), si) for j in range(1, frames)]
@@ -245,20 +232,17 @@
                 member = 2 * pair + at
                 pl.when(member != group)(functools.partial(query_wait, h, member))
 
-                @pl.when(jnp.logical_and(passes, member == end_from))
-                def _():
-                    query_on(h).start()
-
             unit(h, pair)
 
-            @pl.when(jnp.logical_and(k == 0, h + 1 < heads))
-            def _():
+            if k == 0 and h + 1 < heads:
                 pass_on(h + 1)
 
-        each(size, step)
+        for k in range(size):
+            step(k)
 
     pass_on(0)
-    each(heads, head)
+    for h in range(heads):
+        head(h)
 
     for member in range(members):
         lse_out[member] = lse_cols[member].T[: lse_out.shape[1]]
@@ -311,10 +295,8 @@
         for j in range(frames + 1):
             forward(h, j).wait_send()
         for j in range(1, members):
-            wanted, copy = query_copy(h, j)
-            pl.when(wanted)(copy.wait_send)
+            query_copy(h, j).wait_send()
             share_copy(h, lax.rem(group + j, members)).wait_send()
-        pl.when(passes)(query_on(h).wait_send)
 
     each(heads, sent)
     for j in range(1, members):

time: 39 us -> 37.3 us (0.956)
  Pallas kernels: 34.8 us -> 33.1 us
    pallas_call x1, Pallas kernels: 34.8 us -> 33.1 us  [body(): pl.pallas_call(functools.partial(attend, frames, members, heads), out_sha...]
where the time goes in v8:
time: 37.3 us; the launch traced here: 37.1 us
  Pallas kernels  33.1 us (89%)
  local copies, waits for them, and re-layouts  3.92 us (11%)
    pallas_call x1, Pallas kernels, body(): pl.pallas_call(functools.partial(attend, frames, members, heads), out_sha...  33.1 us
    unnamed x9, local copies, waits for them, and re-layouts  3.92 us

profile of v8, /device:TPU:0, one launch (start us, length us, event | category | flops | bytes accessed | tf_op | source)
XLA Modules:
  0.0 37.1 jit_solution(6573877847819462306)
XLA Ops:
  0.0 1.0 %copy.11 = bf16[128,4,384]{2,0,1:T(8,128)(2,1)S(1)} copy(bf16[128,4,384]{2,1,0:T(4,128)(2,1)} %param.5) | data formatting | bytes 786432 | tf_op args[0]
  1.0 0.0 copy-start
  1.1 1.6 %copy.10 = bf16[1,128,16,256]{3,1,2,0:T(8,128)(2,1)S(1)} copy(bf16[1,128,16,256]{3,2,1,0:T(8,128)(2,1)} %param.6) | data formatting | bytes 2097152 | tf_op args[1]
  2.6 0.0 copy-start.1
  2.6 0.0 copy-start.2
  2.7 0.0 copy-done
  2.7 0.6 %copy-done.1 = s32[4]{0:T(128)S(1)} copy-done((s32[4]{0:T(128)S(1)}, s32[4]{0:T(128)}, u32[]{:S(2)}) %copy-start.1) | copy-done | bytes 40
  3.3 0.0 copy-done.2
  3.3 33.1 %shard_map.55 = bf16[128,512]{1,0:T(8,128)(2,1)S(1)} custom-call(s32[4]{0:T(128)S(1)} %copy-done.1, s32[8]{0:T(128)S(1)} %copy-done.2, s32[8,8]{1,0:T(8,128)S(1)} %copy-done, bf16[16,128,256]{2,1,0:T(8,128)(2,1)S(1)} %bitcast.8, bf16[4,128,384]{2,1,0:T(8,128)(2,1)S(1)} %bitcast.9), custom_call_target="tpu_custom_call" | custom-call | tf_op jit(solution)/shard_map/pallas_call | solution.py:316
  36.4 0.7 %copy.13 = bf16[128,512]{1,0:T(8,128)(2,1)} copy(bf16[128,512]{1,0:T(8,128)(2,1)S(1)} %shard_map.55) | data formatting | bytes 262144
Async XLA Ops:
  1.0 1.6 %copy-start = (s32[8,8]{1,0:T(8,128)S(1)}, s32[8,8]{1,0:T(8,128)}, u32[]{:S(2)}) copy-start(s32[8,8]{1,0:T(8,128)} %lists_ref.1) | copy-start | bytes 772
  2.6 0.7 %copy-start.1 = (s32[4]{0:T(128)S(1)}, s32[4]{0:T(128)}, u32[]{:S(2)}) copy-start(s32[4]{0:T(128)} %rank_ref.1) | copy-start | bytes 52
  2.6 0.7 %copy-start.2 = (s32[8]{0:T(128)S(1)}, s32[8]{0:T(128)}, u32[]{:S(2)}) copy-start(s32[8]{0:T(128)} %depth_ref.1) | copy-start | bytes 100

commit v9 on v3

--- a/solution.py
+++ b/solution.py
@@ -60,9 +60,6 @@
     size = members // 2
     half = group // size
     place = group - half * size
-    passes = jnp.logical_or(group == 1, group == members - 2)
-    end_from = jnp.where(group == 1, members - 1, 0)
-    end_to = members - 1 - end_from
 
     def frame_at(slot):
         return lax.rem(fi + slot, frames)
@@ -131,21 +128,12 @@
 
     def query_copy(h, j):
         to = lax.rem(group + j, members)
-        return jnp.abs(to - group) != members - 1, remote(
+        return remote(
             own_query(h),
             queries.at[h, group],
             query_send.at[h, j],
             query_recv.at[h, group],
             device_of(to),
-        )
-
-    def query_on(h):
-        return remote(
-            queries.at[h, end_from],
-            queries.at[h, end_from],
-            query_send.at[h, 0],
-            query_recv.at[h, end_from],
-            device_of(end_to),
         )
 
     def query_wait(h, member):
@@ -163,8 +151,7 @@
 
     def start_query(h):
         for j in range(1, members):
-            wanted, copy = query_copy(h, j)
-            pl.when(wanted)(copy.start)
+            query_copy(h, j).start()
 
     barrier = pltpu.get_barrier_semaphore()
     partners = [(frame_at(j), si) for j in range(1, frames)]
@@ -174,7 +161,7 @@
         pl.semaphore_signal(barrier, inc=1, device_id=partner, device_id_type=MESH)
     pl.semaphore_wait(barrier, len(partners))
 
-    ahead = min(2, heads)
+    ahead = heads
     for h in range(ahead):
         start_past(h)
         start_query(h)
@@ -274,16 +261,9 @@
         for k in range(size // 2):
             early(h, half * (size // 2) + k)
 
-        @pl.when(passes)
-        def _():
-            query_wait(h, end_from)
-            query_on(h).start()
-
         for i in range(size):
             member = (1 - half) * size + i
-            pl.when(jnp.logical_not(jnp.logical_and(passes, member == end_from)))(
-                functools.partial(query_wait, h, member)
-            )
+            query_wait(h, member)
         if h + ahead < heads:
             start_query(h + ahead)
         for k in range(size // 2):
@@ -376,10 +356,8 @@
         for j in range(2):
             early_forward(h, j).wait_send()
         for j in range(1, members):
-            wanted, copy = query_copy(h, j)
-            pl.when(wanted)(copy.wait_send)
+            query_copy(h, j).wait_send()
             share_copy(h, lax.rem(group + j, members)).wait_send()
-        pl.when(passes)(query_on(h).wait_send)
     for j in range(1, members):
         lse_copy(j).wait_send()
 

time: 40.4 us -> 39.3 us (0.973)
  Pallas kernels: 36.3 us -> 35.2 us
    pallas_call x1, Pallas kernels: 36.3 us -> 35.2 us  [body(): pl.pallas_call(functools.partial(attend, frames, members, heads), out_sha...]
where the time goes in v9:
time: 39.3 us; the launch traced here: 39.2 us
  Pallas kernels  35.2 us (90%)
  local copies, waits for them, and re-layouts  3.92 us (10%)
    pallas_call x1, Pallas kernels, body(): pl.pallas_call(functools.partial(attend, frames, members, heads), out_sha...  35.2 us
    unnamed x9, local copies, waits for them, and re-layouts  3.92 us

profile of v9, /device:TPU:0, one launch (start us, length us, event | category | flops | bytes accessed | tf_op | source)
XLA Modules:
  0.0 39.2 jit_solution(4833687079873837701)
XLA Ops:
  0.0 1.0 %copy.11 = bf16[128,4,384]{2,0,1:T(8,128)(2,1)S(1)} copy(bf16[128,4,384]{2,1,0:T(4,128)(2,1)} %param.5) | data formatting | bytes 786432 | tf_op args[0]
  1.0 0.0 copy-start
  1.1 1.6 %copy.10 = bf16[1,128,16,256]{3,1,2,0:T(8,128)(2,1)S(1)} copy(bf16[1,128,16,256]{3,2,1,0:T(8,128)(2,1)} %param.6) | data formatting | bytes 2097152 | tf_op args[1]
  2.6 0.0 copy-start.1
  2.6 0.0 copy-start.2
  2.7 0.0 copy-done
  2.7 0.6 %copy-done.1 = s32[4]{0:T(128)S(1)} copy-done((s32[4]{0:T(128)S(1)}, s32[4]{0:T(128)}, u32[]{:S(2)}) %copy-start.1) | copy-done | bytes 40
  3.3 0.0 copy-done.2
  3.3 35.2 %shard_map.55 = bf16[128,512]{1,0:T(8,128)(2,1)S(1)} custom-call(s32[4]{0:T(128)S(1)} %copy-done.1, s32[8]{0:T(128)S(1)} %copy-done.2, s32[8,8]{1,0:T(8,128)S(1)} %copy-done, bf16[16,128,256]{2,1,0:T(8,128)(2,1)S(1)} %bitcast.8, bf16[4,128,384]{2,1,0:T(8,128)(2,1)S(1)} %bitcast.9), custom_call_target="tpu_custom_call" | custom-call | tf_op jit(solution)/shard_map/pallas_call | solution.py:377
  38.5 0.7 %copy.13 = bf16[128,512]{1,0:T(8,128)(2,1)} copy(bf16[128,512]{1,0:T(8,128)(2,1)S(1)} %shard_map.55) | data formatting | bytes 262144
Async XLA Ops:
  1.0 1.6 %copy-start = (s32[8,8]{1,0:T(8,128)S(1)}, s32[8,8]{1,0:T(8,128)}, u32[]{:S(2)}) copy-start(s32[8,8]{1,0:T(8,128)} %lists_ref.1) | copy-start | bytes 772
  2.6 0.7 %copy-start.1 = (s32[4]{0:T(128)S(1)}, s32[4]{0:T(128)}, u32[]{:S(2)}) copy-start(s32[4]{0:T(128)} %rank_ref.1) | copy-start | bytes 52
  2.6 0.7 %copy-start.2 = (s32[8]{0:T(128)S(1)}, s32[8]{0:T(128)}, u32[]{:S(2)}) copy-start(s32[8]{0:T(128)} %depth_ref.1) | copy-start | bytes 100
